TPU v7x, 512 devices: a whole 4x4x16 slice. The times are simulated.
512 devices in a mesh: grp: 16 (over z_lo, x), feat: 32 (over y, z_hi, core).
Axes of the slice: x: 4, y: 4, z: 16 (z_hi: 4, z_lo: 4; z = z_hi * 4 + z_lo), core: 2. Of those that a mesh axis runs over, the one named last changes fastest.
Arguments:
- features: bfloat16 [16384, 768], P('grp', 'feat'), may hold values from -6 to 6
- adjacency: bfloat16 [128, 128, 256], P('grp'), may hold values from 0 to 0.119628906
- offsets: int32 [128], P('grp'), may hold values from 0 to 1024, as said below
- live: int32 [128], P('grp'), may hold values 0 or 1
- w_self: bfloat16 [768, 1024], P('feat'), may hold values from -0.21875 to 0.21875
- w_neigh: bfloat16 [768, 1024], P('feat'), may hold values from -0.21875 to 0.21875
- bias: float32 [1024], replicated, may hold values from -3 to 3
- targets: bfloat16 [1024, 16384], P('feat', 'grp'), may hold values from -6 to 6
Outputs:
- hidden: bfloat16 [1024, 16384], P('feat', 'grp')
- grad_self: float32 [768, 1024], P('feat')
- grad_neigh: float32 [768, 1024], P('feat')
- grad_bias: float32 [1024], replicated
Inputs may be any that keep to these rules, and one draw needn't show every extreme that they name: `offsets`: tile k of a range (counted from 0) starts between k * 128 and k * 128 + 128; the first tile of range 0 starts at 0 and the last tile of the last range at 1024.
All inputs are finite; a program needn't handle non-finite values. No bound on the sum of `live` on one device may be relied on, other than what follows from the above.
Results may differ from a plain program's by a relative error of at most 0.0039.
Values may be sent and summed in bfloat16 or wider, within the bound.
A program may use at most 64 MiB of HBM per device.

v0:
```python
import math

import jax
import jax.numpy as jnp
from jax import lax
from jax.sharding import PartitionSpec as P

BAND = 256
HALO = 128


def with_halo(cells, sides, width):
    for axis, dim in sides:
        count = lax.axis_size(axis)
        ends = count - 1
        head = lax.slice_in_dim(cells, 0, width, axis=dim)
        tail = lax.slice_in_dim(cells, cells.shape[dim] - width, cells.shape[dim], axis=dim)
        cells = jnp.concatenate(
            [
                lax.ppermute(tail, axis, [(i, (i + 1) % count) for i in range(ends)]),
                cells,
                lax.ppermute(head, axis, [((i + 1) % count, i) for i in range(ends)]),
            ],
            axis=dim,
        )
    return cells


def slope(values):
    logistic = jax.nn.sigmoid(values)
    return logistic * (1.0 + values * (1.0 - logistic))


def project(weight, nodes):
    return lax.dot_general(
        weight, nodes, (((0,), (1,)), ((), ())), preferred_element_type=jnp.float32
    )


def outer_rows(nodes, delta_block):
    return lax.dot_general(
        nodes.astype(jnp.float32),
        delta_block,
        (((0,), (1,)), ((), ())),
        precision=lax.Precision.HIGHEST,
        preferred_element_type=jnp.float32,
    )


def shards(features, adjacency, offsets, live, w_self, w_neigh, bias, targets):
    row_count = features.shape[0]
    width = features.shape[1]
    extended = with_halo(features, (("grp", 0),), HALO)
    columns = offsets[:, None] + jnp.arange(BAND, dtype=jnp.int32)[None, :]
    windows = extended[columns]
    summed = jnp.einsum("tij,tjd->tid", adjacency, windows, preferred_element_type=jnp.float32)
    summed = summed * live.astype(jnp.float32)[:, None, None]
    neighbour = summed.reshape(row_count, width).astype(jnp.bfloat16)
    hid_width = w_self.shape[1]
    own_cols = hid_width // lax.axis_size("feat")
    first_col = lax.axis_index("feat") * own_cols
    bias_own = lax.dynamic_slice_in_dim(bias, first_col, own_cols, 0)
    scaling = math.sqrt(row_count * lax.axis_size("grp"))
    pre = (
        lax.psum_scatter(
            project(w_self, features) + project(w_neigh, neighbour),
            "feat",
            scatter_dimension=0,
            tiled=True,
        )
        + bias_own[:, None]
    )
    act = jax.nn.silu(pre)
    hidden = act.astype(jnp.bfloat16)
    delta = (act - targets.astype(jnp.float32)) * slope(pre) / scaling
    piece = lax.all_gather(delta, "feat", axis=0, tiled=True)
    grad_self, grad_neigh, grad_bias = lax.psum(
        (outer_rows(features, piece), outer_rows(neighbour, piece), jnp.sum(piece, axis=1)), "grp"
    )
    return (hidden, grad_self, grad_neigh, grad_bias)


def solution(mesh):
    in_specs = (
        P("grp", "feat"),
        P("grp", None, None),
        P("grp"),
        P("grp"),
        P("feat", None),
        P("feat", None),
        P(),
        P("feat", "grp"),
    )
    out_specs = (P("feat", "grp"), P("feat", None), P("feat", None), P())
    return jax.shard_map(shards, mesh=mesh, in_specs=in_specs, out_specs=out_specs, check_vma=False)
```

profile of v0, /device:TPU:8, one launch (start us, length us, event | category | flops | bytes accessed | tf_op | source)
XLA Modules:
  0.0 442.8 jit_solution(15548932220043282292)
XLA Ops:
  7.2 0.0 copy-start
  7.2 0.0 copy-start.2
  7.2 0.0 copy-start.5
  7.2 0.0 reduce-scatter.2.cloned.1.call-start
  7.2 0.8 fusion.10
  8.0 3.4 collective-permute-start
  11.4 1.3 collective-permute-start.1
  12.7 0.7 fusion.9
  13.4 3.5 fusion.11
  16.9 0.0 copy-start.4
  16.9 0.0 copy-done.5
  17.0 0.0 collective-permute-done
  17.0 0.0 collective-permute-done.1
  17.0 0.0 copy-done.2
  17.0 0.2 copy.23
  17.2 6.2 %gather_fusion = bf16[2048,24]{1,0:T(8,128)(2,1)S(1)} fusion(bf16[1280,24]{1,0:T(8,128)(2,1)S(1)} %copy.23, s32[2048]{0:T(1024)S(1)} %broadcast_clamp_fusion), kind=kCustom, calls=%fused_computation | custom fusion | bytes 204800 | tf_op jit(solution)/shard_map/gather | solution.py:55
  23.4 0.0 copy-done
  23.4 0.3 fusion.1
  23.7 0.0 copy-done.4
  23.7 4.9 %bitcast_add_fusion = f32[1024,1024]{1,0:T(8,128)} fusion(f32[1024,1024]{1,0:T(8,128)} %fusion.11, bf16[24,1024]{1,0:T(8,128)(2,1)S(1)} %copy-done.4, bf16[8,3,8,128]{3,2,1,0:T(8,128)(2,1)S(1)} %fusion.1), kind=kOutput, calls=%fused_computation.1 | convolution fusion | flops 51380224 | bytes 8486912 | tf_op jit(solution)/shard_map/dot_general | solution.py:35
  28.6 0.0 copy-start.3
  28.6 0.0 reduce-scatter.2.cloned.1.call-update
  28.7 0.0 all-gather.2.cloned.1.call-start
  28.7 0.8 dynamic_slice.3
  29.5 142.6 %reduce-scatter.2.cloned.1.call-done = f32[32,1024]{1,0:T(8,128)} async-done(((f32[1024,1024]{1,0:T(8,128)}), f32[32,1024]{1,0:T(8,128)}) %reduce-scatter.2.cloned.1.call-update) | async-done | bytes 131088 | tf_op jit(solution)/shard_map/reduce_scatter | solution.py:65
  172.1 0.0 copy-done.3
  172.1 1.7 multiply_multiply_fusion
  173.8 0.0 all-gather.2.cloned.1.call-update
  173.8 0.0 all-reduce.3.cloned.1.call-start
  173.9 92.4 %all-gather.2.cloned.1.call-done = f32[1024,1024]{1,0:T(8,128)} async-done(((f32[32,1024]{1,0:T(8,128)}), f32[1024,1024]{1,0:T(8,128)}) %all-gather.2.cloned.1.call-update) | async-done | bytes 4194320 | tf_op jit(solution)/shard_map/all_gather | solution.py:76
  266.3 0.0 copy-start.1
  266.3 4.9 %fusion.4 = f32[24,1024]{1,0:T(8,128)} fusion(f32[1024,1024]{1,0:T(8,128)} %all-gather.2.cloned.1.call-done, bf16[8,3,8,128]{3,2,1,0:T(8,128)(2,1)S(1)} %fusion.1), kind=kOutput, calls=%fused_computation.11 | convolution fusion | flops 301989888 | bytes 4341760 | tf_op jit(solution)/shard_map/dot_general | solution.py:41
  271.2 0.0 copy-done.1
  271.2 2.6 convolution_bitcast_fusion
  273.9 0.0 all-reduce.3.cloned.1.call-update
  273.9 2.5 reduce_sum.9
  276.3 43.1 %psum.23 = f32[1024]{0:T(1024)} all-reduce(f32[1024]{0:T(1024)S(1)} %reduce_sum.9), channel_id=1, replica_groups=mesh['grp'=16,'feat'=32] {'grp'}, use_global_device_ids=true, to_apply=%region_4.5 | all-reduce | flops 1024 | bytes 8192 | tf_op jit(solution)/shard_map/psum | solution.py:77
  319.4 113.8 %all-reduce.3.cloned.1.call-done = (f32[24,1024]{1,0:T(8,128)}, f32[24,1024]{1,0:T(8,128)}) async-done(((f32[24,1024]{1,0:T(8,128)}, f32[24,1024]{1,0:T(8,128)}), (f32[24,1024]{1,0:T(8,128)}, f32[24,1024]{1,0:T(8,128)})) %all-reduce.3.cloned.1.call-update) | async-done | bytes 196624 | tf_op jit(solution)/shard_map/psum | solution.py:77
  433.2 1.5 copy.41
  434.7 1.5 copy.42
  (4 shorter events, 0.0 us)
Async XLA Ops:
  7.2 16.3 %copy-start = (bf16[8,128,256]{2,1,0:T(8,128)(2,1)S(1)}, bf16[8,128,256]{2,1,0:T(8,128)(2,1)}, u32[]{:S(2)}) copy-start(bf16[8,128,256]{2,1,0:T(8,128)(2,1)} %param.9) | copy-start | bytes 1572868
  7.2 9.8 %copy-start.2 = (bf16[1024,24]{0,1:T(8,128)(2,1)S(1)}, bf16[1024,24]{0,1:T(8,128)(2,1)}, u32[]{:S(2)}) copy-start(bf16[1024,24]{0,1:T(8,128)(2,1)} %param.8) | copy-start | bytes 147460
  7.2 9.8 %copy-start.5 = (s32[8]{0:T(128)S(1)}, s32[8]{0:T(128)}, u32[]{:S(2)}) copy-start(s32[8]{0:T(128)} %param.11) | copy-start | bytes 100
  7.2 164.9 %reduce-scatter.2.cloned.1.call-start = ((), (), s32[]{:S(2)}) async-start(), calls=%async_computation.1 | async-start | bytes 4325376 | tf_op jit(solution)/shard_map/reduce_scatter | solution.py:65
  8.0 9.0 %collective-permute-start = (bf16[128,24]{0,1:T(8,128)(2,1)S(1)}, bf16[128,24]{0,1:T(8,128)(2,1)S(1)}, u32[]{:S(2)}, u32[]{:S(2)}) collective-permute-start(bf16[128,24]{0,1:T(8,128)(2,1)S(1)} %get-tuple-element.8), channel_id=1, source_target_pairs={{0,32},{32,64},{64,96},{96,128},{128,160},{160,192},{192,224},{224... | collective-permute-start | bytes 18440 | tf_op jit(solution)/shard_map/ppermute | solution.py:20
  11.4 5.6 %collective-permute-start.1 = (bf16[128,24]{0,1:T(8,128)(2,1)S(1)}, bf16[128,24]{0,1:T(8,128)(2,1)S(1)}, u32[]{:S(2)}, u32[]{:S(2)}) collective-permute-start(bf16[128,24]{0,1:T(8,128)(2,1)S(1)} %get-tuple-element.9), channel_id=1, source_target_pairs={{32,0},{64,32},{96,64},{128,96},{160,128},{192,160},{224,192},{256... | collective-permute-start | bytes 18440 | tf_op jit(solution)/shard_map/ppermute | solution.py:22
  16.9 6.8 %copy-start.4 = (bf16[24,1024]{1,0:T(8,128)(2,1)S(1)}, bf16[24,1024]{1,0:T(8,128)(2,1)}, u32[]{:S(2)}) copy-start(bf16[24,1024]{1,0:T(8,128)(2,1)} %param.13) | copy-start | bytes 147460
  28.6 143.5 %copy-start.3 = (bf16[32,1024]{1,0:T(8,128)(2,1)S(1)}, bf16[32,1024]{1,0:T(8,128)(2,1)}, u32[]{:S(2)}) copy-start(bf16[32,1024]{1,0:T(8,128)(2,1)} %param.15) | copy-start | bytes 196612
  28.7 237.6 %all-gather.2.cloned.1.call-start = ((), (), s32[]{:S(2)}) async-start(), calls=%async_computation.2 | async-start | bytes 4325376 | tf_op jit(solution)/shard_map/all_gather | solution.py:76
  173.8 259.3 %all-reduce.3.cloned.1.call-start = ((), (), s32[]{:S(2)}) async-start(), calls=%async_computation.3 | async-start | bytes 393216 | tf_op jit(solution)/shard_map/psum | solution.py:77
  266.3 4.9 %copy-start.1 = (f32[1024,1024]{1,0:T(8,128)S(1)}, f32[1024,1024]{1,0:T(8,128)}, u32[]{:S(2)}) copy-start(f32[1024,1024]{1,0:T(8,128)} %all-gather.2.cloned.1.call-done) | copy-start | bytes 12582916
Sparse Core Ops, SparseCore 0:
  28.8 143.2 reduce-scatter.1
  175.7 90.5 all-gather.1
  274.0 159.1 all-reduce.2
where the time goes:
time: 443 us
  waiting for transfers between devices  349 us (79%)
  blocking collectives  43.1 us (10%)
  matrix products  16.3 us (4%)
  between operations  13.9 us (3%)
  local copies, waits for them, and re-layouts  11 us (2%)
  other arithmetic  4.91 us (1%)
  starting transfers between devices  4.8 us (1%)
    reduce_scatter x1, waiting for transfers between devices, shards(): lax.psum_scatter(project(w_self, features) + project(w_neigh, neighbour),...  143 us
    psum x1, waiting for transfers between devices, shards(): lax.psum((outer_rows(features, piece), outer_rows(neighbour, piece), jnp....  114 us
    all_gather x1, waiting for transfers between devices, shards(): piece = lax.all_gather(delta, 'feat', axis=0, tiled=True)  92.4 us
    psum x1, blocking collectives, shards(): lax.psum((outer_rows(features, piece), outer_rows(neighbour, piece), jnp....  43.1 us
  transfers between devices with their start and end apart: 5, of which 3 were waited for; matrix products, arithmetic and copies ran while one was open for 2% of the time, Pallas kernels for 0%

commit v1 on v0

v1 whole, which is shorter than its diff:
```python
import jax
import jax.numpy as jnp
from jax import lax
from jax.experimental import pallas as pl
from jax.experimental.pallas import tpu as pltpu
from jax.sharding import PartitionSpec as P

F32 = jnp.float32
BF16 = jnp.bfloat16
MESH = pl.DeviceIdType.MESH

COLS = 24
PAIR = 48
COLUMN = 4 * PAIR
HALF = 640
PART_A = 384
PART_B = HALF - PART_A
TILE = 128
SENDS = 96
RECVS = 64


def mod4(value):
    return lax.rem(value + 4, 4)


def kernel(
    feat_h, adj_h, off_h, live_h, ws_h, wn_h, bias_h, tgt_h,
    out,
    feat, adj, off, live, ws, wn, bias, tgt,
    wide, stage, xg, nb, band, wsend, wg, wt, pre_acc, rsend, ra, rbs, rb, fg, fin,
    in_sem, send_sem, recv_sem,
):
    loads = [
        pltpu.make_async_copy(src, dst, in_sem.at[i])
        for i, (src, dst) in enumerate(
            [(feat_h, feat), (ws_h, ws), (wn_h, wn), (adj_h, adj), (off_h, off), (live_h, live),
             (bias_h, bias), (tgt_h, tgt)]
        )
    ]
    for load in loads:
        load.start()

    g = lax.axis_index("grp")
    f = lax.axis_index("feat")
    c = lax.rem(f, 2)
    p = lax.div(f, 2)
    y = lax.div(p, 4)
    zh = lax.rem(p, 4)
    x = lax.rem(g, 4)
    zl = lax.div(g, 4)
    other = 1 - c
    sign = 1 - 2 * c

    def device(group, chip, core):
        return (group, chip * 2 + core)

    partner = device(g, p, other)
    y_fwd = device(g, mod4(y + sign) * 4 + zh, c)
    y_bwd = device(g, mod4(y - sign) * 4 + zh, c)
    y_far = device(g, mod4(y + 2) * 4 + zh, c)
    z_fwd = device(g, y * 4 + mod4(zh + sign), c)
    z_bwd = device(g, y * 4 + mod4(zh - sign), c)
    stays = jnp.logical_and(zh == zl, jnp.logical_and(x == 0, y == 0))

    barrier = pltpu.get_barrier_semaphore()

    def tell(target):
        pl.semaphore_signal(barrier, inc=1, device_id=target, device_id_type=MESH)

    @pl.when(jnp.logical_and(c == 0, g > 0))
    def _():
        tell(device(g - 1, p, 0))
        tell(device(g - 1, p, 1))

    @pl.when(jnp.logical_and(c == 1, g < 15))
    def _():
        tell(device(g + 1, p, 0))
        tell(device(g + 1, p, 1))

    for target in (z_fwd, z_bwd, y_fwd, y_bwd, y_far, partner):
        tell(target)

    w_src_y = mod4(y + x)
    w_dst_y = mod4(y - x)
    r_chip = mod4(x - y) * 4 + zl
    for step in range(1, 4):
        tell(device(g, w_src_y * 4 + mod4(zh + step), c))
        tell(device(mod4(zl + step) * 4 + y, r_chip, c))

    @pl.when(x != 0)
    def _():
        tell(device(g, w_src_y * 4 + zh, c))

    @pl.when(jnp.logical_not(stays))
    def _():
        tell(device(zl * 4 + y, r_chip, c))

    def tell_far(step, carry):
        tell(device(lax.rem(g + step, 16), p, c))
        return carry

    lax.fori_loop(1, 16, tell_far, 0)

    loads[0].wait()
    wide[...] = feat[...].astype(F32)

    @pl.when(c == 0)
    def _():
        stage[0:COLS, TILE:HALF] = wide[:, 0:512]

        @pl.when(g == 0)
        def _():
            stage[:, 0:TILE] = jnp.zeros((PAIR, TILE), F32)

    @pl.when(c == 1)
    def _():
        stage[COLS:PAIR, 0:512] = wide[:, 512:1024]

        @pl.when(g == 15)
        def _():
            stage[:, 512:HALF] = jnp.zeros((PAIR, TILE), F32)

    waits = (
        6 + 3 + 3 + 15
        + (x != 0).astype(jnp.int32)
        + jnp.logical_not(stays).astype(jnp.int32)
        + (g < 15).astype(jnp.int32)
        + (g > 0).astype(jnp.int32)
    )
    pl.semaphore_wait(barrier, waits)

    used = [0, 0]
    sent = []

    def slot(which, count=1):
        used[which] += count
        return used[which] - count

    def remote(src, dst, target, send, recv):
        return pltpu.make_async_remote_copy(
            src_ref=src, dst_ref=dst, send_sem=send_sem.at[send], recv_sem=recv_sem.at[recv],
            device_id=target, device_id_type=MESH,
        )

    def copy(src, dst, target, recv):
        made = remote(src, dst, target, slot(0), recv)
        made.start()
        sent.append(made)

    def await_bytes(ref, recv):
        pltpu.make_async_copy(ref, ref, recv_sem.at[recv]).wait()

    own_rows = pl.ds(pl.multiple_of(c * COLS, 8), COLS)
    other_rows = pl.ds(pl.multiple_of(other * COLS, 8), COLS)
    r_left, r_right, r_swap = slot(1, 2), slot(1, 2), slot(1)
    halo_up = remote(
        wide.at[:, 896:1024], stage.at[own_rows, 0:TILE], device(g + 1, p, 0), slot(0), r_left + c
    )
    halo_down = remote(
        wide.at[:, 0:TILE], stage.at[own_rows, 512:HALF], device(g - 1, p, 1), slot(0), r_right + c
    )

    @pl.when(g < 15)
    def _():
        halo_up.start()

    @pl.when(g > 0)
    def _():
        halo_down.start()

    copy(
        wide.at[:, pl.ds(pl.multiple_of(other * 512, 128), 512)],
        stage.at[own_rows, pl.ds(pl.multiple_of(c * TILE, 128), 512)],
        partner, r_swap,
    )

    loads[1].wait()
    loads[2].wait()
    lane = lax.broadcasted_iota(jnp.int32, (COLS, 128), 1)
    pad = jnp.zeros((32 - COLS, 128), F32)
    for pair in range(8):
        s_tile = ws[:, pair * 128:(pair + 1) * 128].astype(F32)
        n_tile = wn[:, pair * 128:(pair + 1) * 128].astype(F32)
        low = jnp.where(lane < 64, s_tile, pltpu.roll(n_tile, 64, 1))
        high = jnp.where(lane < 64, pltpu.roll(s_tile, 64, 1), n_tile)
        wsend[2 * pair] = jnp.concatenate([low, pad], 0).astype(BF16)
        wsend[2 * pair + 1] = jnp.concatenate([high, pad], 0).astype(BF16)

    r_w1 = slot(1, 4)
    for step in range(1, 4):
        chip = w_dst_y * 4 + mod4(zh + step)
        copy(wsend.at[chip], wg.at[c, p], device(g, chip, c), r_w1 + step)
    chip0 = w_dst_y * 4 + zh
    w_zero = remote(wsend.at[chip0], wg.at[c, p], device(g, chip0, c), slot(0), r_w1)

    @pl.when(x != 0)
    def _():
        w_zero.start()

    @pl.when(x == 0)
    def _():
        wg[c, p] = wsend[chip0]

    for load in loads[3:6]:
        load.wait()
    for tile in range(8):
        dense = adj[tile].astype(F32)
        padded = jnp.concatenate([dense, jnp.zeros((TILE, TILE), F32)], 1)
        moved = pltpu.roll(padded, off[tile] - tile * TILE, 1)
        band[tile] = (moved * live[tile].astype(F32)).astype(BF16)

    await_bytes(stage.at[other_rows, pl.ds(pl.multiple_of(other * TILE, 128), 512)], r_swap)

    @pl.when(jnp.logical_and(c == 0, g > 0))
    def _():
        await_bytes(stage.at[0:COLS, 0:TILE], r_left)
        await_bytes(stage.at[COLS:PAIR, 0:TILE], r_left + 1)

    @pl.when(jnp.logical_and(c == 1, g < 15))
    def _():
        await_bytes(stage.at[0:COLS, 512:HALF], r_right)
        await_bytes(stage.at[COLS:PAIR, 512:HALF], r_right + 1)

    def block(by, bz, part):
        rows = pl.ds(pl.multiple_of((mod4(bz) * 4 + mod4(by)) * PAIR, 16), PAIR)
        start = {"all": 0, "a": 0, "b": PART_A}[part]
        width = {"all": HALF, "a": PART_A, "b": PART_B}[part]
        return xg.at[rows, pl.ds(pl.multiple_of(c * HALF + start, 128), width)]

    block(y, zh, "all")[...] = stage[...].astype(BF16)

    r_pair = slot(1, 4)

    def forward(by, bz, part, target, recv):
        view = block(by, bz, part)
        copy(view, view, target, recv)

    def share(by, bz, part):
        forward(by, bz, part, partner, r_pair + mod4(bz))

    r_z1 = slot(1, 4)
    r_z2 = slot(1, 2)
    r_y1 = slot(1, 6)
    r_y2 = slot(1, 6)
    r_y3 = slot(1, 6)

    def column(number):
        return zh + sign * (0, -1, 1)[number]

    def send_y1(number):
        forward(y, column(number), "all", y_fwd, r_y1 + 2 * number)
        forward(y, column(number), "all", y_bwd, r_y1 + 2 * number + 1)

    def take_y1(number):
        bz = column(number)
        await_bytes(block(y - sign, bz, "all"), r_y1 + 2 * number)
        forward(y - sign, bz, "a", y_fwd, r_y2 + 2 * number)
        await_bytes(block(y + sign, bz, "all"), r_y1 + 2 * number + 1)
        forward(y + sign, bz, "b", y_bwd, r_y2 + 2 * number + 1)
        share(y - sign, bz, "all")
        share(y + sign, bz, "all")

    def take_y2(number):
        bz = column(number)
        await_bytes(block(y + 2, bz, "a"), r_y2 + 2 * number)
        share(y + 2, bz, "a")
        await_bytes(block(y + 2, bz, "b"), r_y2 + 2 * number + 1)
        share(y + 2, bz, "b")

    def send_y3(part):
        first = r_y3 + (0 if part == "a" else 3)
        forward(y, zh + 2, part, y_fwd, first)
        forward(y, zh + 2, part, y_bwd, first + 1)
        forward(y, zh + 2, part, y_far, first + 2)
        share(y, zh + 2, part)

    def take_y3(part):
        first = r_y3 + (0 if part == "a" else 3)
        for offset, by in enumerate((y - sign, y + sign, y + 2)):
            await_bytes(block(by, zh + 2, part), first + offset)
            share(by, zh + 2, part)

    forward(y, zh, "a", z_fwd, r_z1)
    forward(y, zh, "b", z_bwd, r_z1 + 1)
    forward(y, zh, "b", z_fwd, r_z1 + 2)
    forward(y, zh, "a", z_bwd, r_z1 + 3)
    send_y1(0)
    share(y, zh, "all")

    for step in range(1, 4):
        await_bytes(wg.at[c, w_src_y * 4 + mod4(zh + step)], r_w1 + 4 - step)

    @pl.when(x != 0)
    def _():
        await_bytes(wg.at[c, w_src_y * 4 + zh], r_w1)

    r_w2 = slot(1, 4)
    part_w = wg.at[c, pl.ds(w_src_y * 4, 4)]
    for step in range(1, 4):
        copy(part_w, part_w, device(g - x + mod4(x + step), p, c), r_w2 + step)

    take_y1(0)

    for step in range(1, 4):
        await_bytes(wg.at[c, pl.ds(mod4(y + x - step) * 4, 4)], r_w2 + step)
    r_w3 = slot(1)
    copy(wg.at[c], wg.at[c], partner, r_w3)
    take_y2(0)

    await_bytes(block(y, zh - sign, "a"), r_z1)
    forward(y, zh - sign, "a", z_fwd, r_z2)
    await_bytes(block(y, zh + sign, "b"), r_z1 + 1)
    forward(y, zh + sign, "b", z_bwd, r_z2 + 1)

    await_bytes(wg.at[other], r_w3)
    for col in range(4):
        rows = []
        for row in range(4):
            for core in range(2):
                rows.append(wg[core, row * 4 + col].astype(F32)[0:COLS])
        wt[col] = jnp.concatenate(rows, 0).T.astype(BF16)

    await_bytes(block(y, zh - sign, "b"), r_z1 + 2)
    send_y1(1)
    await_bytes(block(y, zh + sign, "a"), r_z1 + 3)
    send_y1(2)
    share(y, zh - sign, "all")
    share(y, zh + sign, "all")

    loads[6].wait()
    spot = lax.broadcasted_iota(jnp.int32, (32, 1024), 1)
    row = lax.broadcasted_iota(jnp.int32, (32, 1024), 0)
    bias_own = jnp.sum(
        jnp.where(spot == row + f * 32, jnp.broadcast_to(bias[...], (32, 1024)), 0.0),
        axis=1, keepdims=True,
    )
    pre_acc[...] = jnp.broadcast_to(bias_own, (32, 1024))

    def compute(bz):
        col = mod4(bz)
        rows = pl.ds(pl.multiple_of(col * COLUMN, 16), COLUMN)
        await_bytes(xg.at[rows, pl.ds(pl.multiple_of(other * HALF, 128), HALF)], r_pair + col)
        for tile in range(8):
            nb[rows, tile * TILE:(tile + 1) * TILE] = lax.dot_general(
                xg[rows, tile * TILE:tile * TILE + 3 * TILE], band[tile],
                (((1,), (1,)), ((), ())), preferred_element_type=F32,
            ).astype(BF16)
        ws_t = wt[col, pl.ds(pl.multiple_of(c * 32, 16), 32), :]
        wn_t = wt[col, pl.ds(pl.multiple_of(64 + c * 32, 16), 32), :]
        pre_acc[...] += (
            jnp.dot(ws_t, xg[rows, TILE:TILE + 1024], preferred_element_type=F32)
            + jnp.dot(wn_t, nb[rows, :], preferred_element_type=F32)
        )

    compute(zh)
    take_y1(1)
    take_y1(2)
    await_bytes(block(y, zh + 2, "a"), r_z2)
    send_y3("a")
    await_bytes(block(y, zh + 2, "b"), r_z2 + 1)
    send_y3("b")
    take_y2(1)
    take_y2(2)
    compute(zh - 1)
    take_y3("a")
    take_y3("b")
    compute(zh + 1)
    compute(zh + 2)

    loads[7].wait()
    pre = pre_acc[...]
    gate = jax.nn.sigmoid(pre)
    act = pre * gate
    out[0:32] = act
    delta = (act - tgt[...].astype(F32)) * (gate * (1.0 + pre * (1.0 - gate))) * (1.0 / 128.0)

    head = delta.astype(BF16)
    rest = (delta - head.astype(F32)).astype(BF16)
    both = jnp.concatenate([head] * 4 + [rest] * 4, 0)
    turn = (((1,), (1,)), ((), ()))
    gs = lax.dot_general(xg[:, TILE:TILE + 1024], both, turn, preferred_element_type=F32)
    gn = lax.dot_general(nb[...], both, turn, preferred_element_type=F32)
    gs = gs[:, 0:128] + gs[:, 128:256]
    gn = gn[:, 0:128] + gn[:, 128:256]
    lanes = lax.broadcasted_iota(jnp.int32, (32, 128), 1)
    bias_term = jnp.sum(delta, axis=1, keepdims=True)
    quarter = lax.div(lax.broadcasted_iota(jnp.int32, (PAIR, 128), 1), 32)
    blank = jnp.zeros((32, 128), F32)

    def packed(grad, row):
        parts = [grad[(col * 4 + row) * PAIR:(col * 4 + row + 1) * PAIR] for col in range(4)]
        low = jnp.where(quarter == 0, parts[0], parts[1])
        high = jnp.where(quarter == 2, parts[2], parts[3])
        return jnp.where(quarter < 2, low, high)

    for row in range(4):
        turned = jnp.concatenate([packed(gs, row), packed(gn, row), blank], 0).T
        for col in range(4):
            rsend[row, col] = jnp.where(lanes == 96, bias_term, turned[col * 32:(col + 1) * 32])

    r_ra = slot(1, 4)
    for step in range(1, 4):
        to_x = mod4(x + step)
        copy(rsend.at[to_x], ra.at[step], device(g - x + to_x, p, c), r_ra + step)

    def with_bias(tile, total):
        first = total.astype(BF16).astype(F32)
        tile = jnp.where(lanes == 96, first, tile)
        return jnp.where(lanes == 97, total - first, tile).astype(BF16)

    for step in range(1, 4):
        await_bytes(ra.at[step], r_ra + step)
    for col in range(4):
        summed = (rsend[x, col] + ra[1, col]) + (ra[2, col] + ra[3, col])
        rbs[col] = with_bias(summed, summed[:, 96:97])

    r_rb = slot(1)
    to_group = zh * 4 + mod4(y + x)
    for step in range(1, 4):
        col = mod4(zh + step)
        copy(rbs.at[col], rb.at[zl], device(to_group, x * 4 + col, c), r_rb)
    r_zero = remote(rbs.at[zh], rb.at[zl], device(to_group, x * 4 + zh, c), slot(0), r_rb)

    @pl.when(jnp.logical_not(stays))
    def _():
        r_zero.start()

    @pl.when(stays)
    def _():
        pltpu.make_async_copy(rbs.at[zh], rb.at[zl], recv_sem.at[r_rb]).start()

    await_bytes(rb, r_rb)
    total = (rb[0].astype(F32) + rb[1].astype(F32)) + (rb[2].astype(F32) + rb[3].astype(F32))
    fg[r_chip, c] = with_bias(total, total[:, 96:97] + total[:, 97:98])

    r_r2 = slot(1)
    mine = fg.at[r_chip, c]
    for step in range(1, 16):
        copy(mine, mine, device(lax.rem(g + step, 16), p, c), r_r2)
    await_bytes(fg.at[pl.ds(0, 15), c], r_r2)
    r_r3 = slot(1)
    copy(fg.at[:, c], fg.at[:, c], partner, r_r3)
    await_bytes(fg.at[:, other], r_r3)
    for part in range(8):
        rows = [fg[2 * part + j, core].astype(F32) for j in range(2) for core in range(2)]
        fin[:, part * 128:(part + 1) * 128] = jnp.concatenate(rows, 0).T
    out[32:56] = fin[pl.ds(pl.multiple_of(c * COLS, 8), COLS), :]
    out[56:80] = fin[pl.ds(pl.multiple_of(PAIR + c * COLS, 8), COLS), :]
    out[80:81] = fin[96:97, :] + fin[97:98, :]

    for made in sent:
        made.wait_send()

    @pl.when(g < 15)
    def _():
        halo_up.wait_send()

    @pl.when(g > 0)
    def _():
        halo_down.wait_send()

    @pl.when(x != 0)
    def _():
        w_zero.wait_send()

    @pl.when(jnp.logical_not(stays))
    def _():
        r_zero.wait_send()

    assert used[0] <= SENDS and used[1] <= RECVS, used


def shards(features, adjacency, offsets, live, w_self, w_neigh, bias, targets):
    vmem = pl.BlockSpec(memory_space=pltpu.VMEM)
    hbm = pl.BlockSpec(memory_space=pltpu.HBM)
    joined = pl.pallas_call(
        kernel,
        out_shape=jax.ShapeDtypeStruct((88, 1024), F32),
        in_specs=[hbm] * 8,
        out_specs=vmem,
        scratch_shapes=[
            pltpu.VMEM((COLS, 1024), BF16),
            pltpu.VMEM((8, TILE, 256), BF16),
            pltpu.SMEM((8,), jnp.int32),
            pltpu.SMEM((8,), jnp.int32),
            pltpu.VMEM((COLS, 1024), BF16),
            pltpu.VMEM((COLS, 1024), BF16),
            pltpu.VMEM((1, 1024), F32),
            pltpu.VMEM((32, 1024), BF16),
            pltpu.VMEM((COLS, 1024), F32),
            pltpu.VMEM((PAIR, HALF), F32),
            pltpu.VMEM((768, 1280), BF16),
            pltpu.VMEM((768, 1024), BF16),
            pltpu.VMEM((8, TILE, 384), BF16),
            pltpu.VMEM((16, 32, 128), BF16),
            pltpu.VMEM((2, 16, 32, 128), BF16),
            pltpu.VMEM((4, 128, COLUMN), BF16),
            pltpu.VMEM((32, 1024), F32),
            pltpu.VMEM((4, 4, 32, 128), F32),
            pltpu.VMEM((4, 4, 32, 128), F32),
            pltpu.VMEM((4, 32, 128), BF16),
            pltpu.VMEM((4, 32, 128), BF16),
            pltpu.VMEM((16, 2, 32, 128), BF16),
            pltpu.VMEM((128, 1024), F32),
            pltpu.SemaphoreType.DMA((8,)),
            pltpu.SemaphoreType.DMA((SENDS,)),
            pltpu.SemaphoreType.DMA((RECVS,)),
        ],
        compiler_params=pltpu.CompilerParams(
            collective_id=0, has_side_effects=True, vmem_limit_bytes=63 * 1024 * 1024
        ),
        cost_estimate=pl.CostEstimate(flops=10**9, bytes_accessed=10**7, transcendentals=32768),
    )(
        features.T, adjacency, offsets, live, w_self, w_neigh, bias.reshape(1, 1024), targets
    )
    return joined[0:32].astype(BF16), joined[32:56], joined[56:80], joined[80]


def solution(mesh):
    in_specs = (
        P("grp", "feat"),
        P("grp", None, None),
        P("grp"),
        P("grp"),
        P("feat", None),
        P("feat", None),
        P(),
        P("feat", "grp"),
    )
    out_specs = (P("feat", "grp"), P("feat", None), P("feat", None), P())
    return jax.shard_map(shards, mesh=mesh, in_specs=in_specs, out_specs=out_specs, check_vma=False)
```

time: 443 us -> 74.8 us (0.17)
  the two profiles are of different devices: /device:TPU:8 before, /device:TPU:1 now
where the time goes in v1:
time: 74.8 us; the launch traced here: 74.6 us
  Pallas kernels  69.4 us (93%)
  local copies, waits for them, and re-layouts  4.52 us (6%)
    pallas_call x1, Pallas kernels, shards(): pl.pallas_call(kernel, out_shape=jax.ShapeDtypeStruct((88, 1024), F32), i...  69.4 us
    slice x3, local copies, waits for them, and re-layouts, shards(): return (joined[0:32].astype(BF16), joined[32:56], joined[56:80], joined[80])  4.52 us

profile of v1, /device:TPU:1, one launch (start us, length us, event | category | flops | bytes accessed | tf_op | source)
XLA Modules:
  0.0 74.6 jit_solution(4177395875975855090)
XLA Ops:
  0.6 69.4 %shard_map.111 = f32[88,1024]{1,0:T(8,128)} custom-call(bf16[24,1024]{1,0:T(8,128)(2,1)} %bitcast.4, bf16[8,128,256]{2,1,0:T(8,128)(2,1)} %adj_h.1, s32[8]{0:T(128)} %off_h.1, s32[8]{0:T(128)} %live_h.1, bf16[24,1024]{1,0:T(8,128)(2,1)} %ws_h.1, bf16[24,1024]{1,0:T(8,128)(2,1)} %wn_h.1, f32[1,1024]{1,0:T(1,128)} %bitcast.5, bf16[32,1024]{1,0:T(8,128)(2,1)} %tgt_h.1), custom_call_target="tpu_custom_call" | custom-call | flops 1000000000 | bytes 10000000 | tf_op jit(solution)/shard_map/pallas_call | solution.py:477
  70.0 1.6 %fusion = (f32[24,1024]{1,0:T(8,128)}, f32[24,1024]{1,0:T(8,128)}) fusion(f32[88,1024]{1,0:T(8,128)} %shard_map.111), kind=kLoop, calls=%fused_computation.1 | loop fusion | bytes 393216 | tf_op jit(solution)/shard_map/slice | solution.py:517
  71.7 1.5 %slice.19 = bf16[32,1024]{1,0:T(8,128)(2,1)} slice(f32[88,1024]{1,0:T(8,128)} %shard_map.111), slice={[0:32], [0:1024]} | slice | bytes 131072 | tf_op jit(solution)/shard_map/slice | solution.py:517
  73.2 1.4 %slice.16 = f32[1,1024]{1,0:T(1,128)} slice(f32[88,1024]{1,0:T(8,128)} %shard_map.111), slice={[80:81], [0:1024]} | slice | bytes 8192 | tf_op jit(solution)/shard_map/slice | solution.py:517

commit v2 on v1

--- a/solution.py
+++ b/solution.py
@@ -26,9 +26,9 @@
 
 def kernel(
     feat_h, adj_h, off_h, live_h, ws_h, wn_h, bias_h, tgt_h,
-    out,
+    hid, gs_o, gn_o, gb_o,
     feat, adj, off, live, ws, wn, bias, tgt,
-    wide, stage, xg, nb, band, wsend, wg, wt, pre_acc, rsend, ra, rbs, rb, fg, fin,
+    wide, stage, xg, nb, band, wsend, wg, wt, pre_acc, rsend, ra, rbs, rb, fg,
     in_sem, send_sem, recv_sem,
 ):
     loads = [
@@ -86,11 +86,14 @@
     r_chip = mod4(x - y) * 4 + zl
     for step in range(1, 4):
         tell(device(g, w_src_y * 4 + mod4(zh + step), c))
-        tell(device(mod4(zl + step) * 4 + y, r_chip, c))
+        tell(device(mod4(zl + step) * 4 + y, r_chip, 0))
+        tell(device(mod4(zl + step) * 4 + y, r_chip, 1))
 
     @pl.when(x != 0)
     def _():
         tell(device(g, w_src_y * 4 + zh, c))
+
+    tell(device(zl * 4 + y, r_chip, other))
 
     @pl.when(jnp.logical_not(stays))
     def _():
@@ -122,7 +125,7 @@
             stage[:, 512:HALF] = jnp.zeros((PAIR, TILE), F32)
 
     waits = (
-        6 + 3 + 3 + 15
+        6 + 3 + 7 + 15
         + (x != 0).astype(jnp.int32)
         + jnp.logical_not(stays).astype(jnp.int32)
         + (g < 15).astype(jnp.int32)
@@ -147,6 +150,11 @@
         made = remote(src, dst, target, slot(0), recv)
         made.start()
         sent.append(made)
+
+    def start_unless(skip, made):
+        @pl.when(jnp.logical_not(skip))
+        def _():
+            made.start()
 
     def await_bytes(ref, recv):
         pltpu.make_async_copy(ref, ref, recv_sem.at[recv]).wait()
@@ -202,33 +210,11 @@
     def _():
         wg[c, p] = wsend[chip0]
 
-    for load in loads[3:6]:
-        load.wait()
-    for tile in range(8):
-        dense = adj[tile].astype(F32)
-        padded = jnp.concatenate([dense, jnp.zeros((TILE, TILE), F32)], 1)
-        moved = pltpu.roll(padded, off[tile] - tile * TILE, 1)
-        band[tile] = (moved * live[tile].astype(F32)).astype(BF16)
-
-    await_bytes(stage.at[other_rows, pl.ds(pl.multiple_of(other * TILE, 128), 512)], r_swap)
-
-    @pl.when(jnp.logical_and(c == 0, g > 0))
-    def _():
-        await_bytes(stage.at[0:COLS, 0:TILE], r_left)
-        await_bytes(stage.at[COLS:PAIR, 0:TILE], r_left + 1)
-
-    @pl.when(jnp.logical_and(c == 1, g < 15))
-    def _():
-        await_bytes(stage.at[0:COLS, 512:HALF], r_right)
-        await_bytes(stage.at[COLS:PAIR, 512:HALF], r_right + 1)
-
     def block(by, bz, part):
         rows = pl.ds(pl.multiple_of((mod4(bz) * 4 + mod4(by)) * PAIR, 16), PAIR)
-        start = {"all": 0, "a": 0, "b": PART_A}[part]
+        start = {"all": 0, "a": other * PART_B, "b": c * PART_A}[part]
         width = {"all": HALF, "a": PART_A, "b": PART_B}[part]
         return xg.at[rows, pl.ds(pl.multiple_of(c * HALF + start, 128), width)]
-
-    block(y, zh, "all")[...] = stage[...].astype(BF16)
 
     r_pair = slot(1, 4)
 
@@ -244,6 +230,25 @@
     r_y1 = slot(1, 6)
     r_y2 = slot(1, 6)
     r_y3 = slot(1, 6)
+
+    await_bytes(stage.at[other_rows, pl.ds(pl.multiple_of(other * TILE, 128), 512)], r_swap)
+    block(y, zh, "a")[...] = stage[:, pl.ds(pl.multiple_of(other * PART_B, 128), PART_A)].astype(BF16)
+    forward(y, zh, "a", z_fwd, r_z1)
+    forward(y, zh, "a", z_bwd, r_z1 + 3)
+
+    @pl.when(jnp.logical_and(c == 0, g > 0))
+    def _():
+        await_bytes(stage.at[0:COLS, 0:TILE], r_left)
+        await_bytes(stage.at[COLS:PAIR, 0:TILE], r_left + 1)
+
+    @pl.when(jnp.logical_and(c == 1, g < 15))
+    def _():
+        await_bytes(stage.at[0:COLS, 512:HALF], r_right)
+        await_bytes(stage.at[COLS:PAIR, 512:HALF], r_right + 1)
+
+    block(y, zh, "b")[...] = stage[:, pl.ds(pl.multiple_of(c * PART_A, 128), PART_B)].astype(BF16)
+    forward(y, zh, "b", z_bwd, r_z1 + 1)
+    forward(y, zh, "b", z_fwd, r_z1 + 2)
 
     def column(number):
         return zh + sign * (0, -1, 1)[number]
@@ -281,12 +286,16 @@
             await_bytes(block(by, zh + 2, part), first + offset)
             share(by, zh + 2, part)
 
-    forward(y, zh, "a", z_fwd, r_z1)
-    forward(y, zh, "b", z_bwd, r_z1 + 1)
-    forward(y, zh, "b", z_fwd, r_z1 + 2)
-    forward(y, zh, "a", z_bwd, r_z1 + 3)
     send_y1(0)
     share(y, zh, "all")
+
+    for load in loads[3:6]:
+        load.wait()
+    for tile in range(8):
+        dense = adj[tile].astype(F32)
+        padded = jnp.concatenate([dense, jnp.zeros((TILE, TILE), F32)], 1)
+        moved = pltpu.roll(padded, off[tile] - tile * TILE, 1)
+        band[tile] = (moved * live[tile].astype(F32)).astype(BF16)
 
     for step in range(1, 4):
         await_bytes(wg.at[c, w_src_y * 4 + mod4(zh + step)], r_w1 + 4 - step)
@@ -312,6 +321,12 @@
     forward(y, zh - sign, "a", z_fwd, r_z2)
     await_bytes(block(y, zh + sign, "b"), r_z1 + 1)
     forward(y, zh + sign, "b", z_bwd, r_z2 + 1)
+    await_bytes(block(y, zh + sign, "a"), r_z1 + 3)
+    send_y1(2)
+    await_bytes(block(y, zh - sign, "b"), r_z1 + 2)
+    send_y1(1)
+    share(y, zh - sign, "all")
+    share(y, zh + sign, "all")
 
     await_bytes(wg.at[other], r_w3)
     for col in range(4):
@@ -320,13 +335,6 @@
             for core in range(2):
                 rows.append(wg[core, row * 4 + col].astype(F32)[0:COLS])
         wt[col] = jnp.concatenate(rows, 0).T.astype(BF16)
-
-    await_bytes(block(y, zh - sign, "b"), r_z1 + 2)
-    send_y1(1)
-    await_bytes(block(y, zh + sign, "a"), r_z1 + 3)
-    send_y1(2)
-    share(y, zh - sign, "all")
-    share(y, zh + sign, "all")
 
     loads[6].wait()
     spot = lax.broadcasted_iota(jnp.int32, (32, 1024), 1)
@@ -354,100 +362,119 @@
         )
 
     compute(zh)
+    take_y1(2)
     take_y1(1)
-    take_y1(2)
     await_bytes(block(y, zh + 2, "a"), r_z2)
     send_y3("a")
     await_bytes(block(y, zh + 2, "b"), r_z2 + 1)
     send_y3("b")
+    take_y2(2)
     take_y2(1)
-    take_y2(2)
     compute(zh - 1)
+    compute(zh + 1)
     take_y3("a")
     take_y3("b")
-    compute(zh + 1)
     compute(zh + 2)
 
     loads[7].wait()
     pre = pre_acc[...]
     gate = jax.nn.sigmoid(pre)
     act = pre * gate
-    out[0:32] = act
+    hid[...] = act.astype(BF16)
     delta = (act - tgt[...].astype(F32)) * (gate * (1.0 + pre * (1.0 - gate))) * (1.0 / 128.0)
 
     head = delta.astype(BF16)
     rest = (delta - head.astype(F32)).astype(BF16)
     both = jnp.concatenate([head] * 4 + [rest] * 4, 0)
     turn = (((1,), (1,)), ((), ()))
-    gs = lax.dot_general(xg[:, TILE:TILE + 1024], both, turn, preferred_element_type=F32)
-    gn = lax.dot_general(nb[...], both, turn, preferred_element_type=F32)
-    gs = gs[:, 0:128] + gs[:, 128:256]
-    gn = gn[:, 0:128] + gn[:, 128:256]
     lanes = lax.broadcasted_iota(jnp.int32, (32, 128), 1)
+    spots = lax.rem(lanes, 64)
     bias_term = jnp.sum(delta, axis=1, keepdims=True)
     quarter = lax.div(lax.broadcasted_iota(jnp.int32, (PAIR, 128), 1), 32)
-    blank = jnp.zeros((32, 128), F32)
-
-    def packed(grad, row):
-        parts = [grad[(col * 4 + row) * PAIR:(col * 4 + row + 1) * PAIR] for col in range(4)]
-        low = jnp.where(quarter == 0, parts[0], parts[1])
-        high = jnp.where(quarter == 2, parts[2], parts[3])
-        return jnp.where(quarter < 2, low, high)
-
+    blank = jnp.zeros((16, 128), F32)
+
+    r_ra = slot(1, 4)
+    terms = []
     for row in range(4):
-        turned = jnp.concatenate([packed(gs, row), packed(gn, row), blank], 0).T
+        spans = [slice((col * 4 + row) * PAIR, (col * 4 + row + 1) * PAIR) for col in range(4)]
+        left = jnp.concatenate(
+            [xg[span, TILE:TILE + 1024] for span in spans] + [nb[span, :] for span in spans], 0
+        )
+        grad = lax.dot_general(left, both, turn, preferred_element_type=F32)
+        grad = grad[:, 0:128] + grad[:, 128:256]
+
+        def packed(first):
+            parts = [grad[first + col * PAIR:first + (col + 1) * PAIR] for col in range(4)]
+            low = jnp.where(quarter == 0, parts[0], parts[1])
+            high = jnp.where(quarter == 2, parts[2], parts[3])
+            return jnp.where(quarter < 2, low, high)
+
+        own_term, nb_term = packed(0), packed(COLUMN)
+        turned = jnp.concatenate(
+            [own_term[0:COLS], nb_term[0:COLS], blank, own_term[COLS:PAIR], nb_term[COLS:PAIR], blank], 0
+        ).T
         for col in range(4):
-            rsend[row, col] = jnp.where(lanes == 96, bias_term, turned[col * 32:(col + 1) * 32])
-
-    r_ra = slot(1, 4)
-    for step in range(1, 4):
-        to_x = mod4(x + step)
-        copy(rsend.at[to_x], ra.at[step], device(g - x + to_x, p, c), r_ra + step)
-
-    def with_bias(tile, total):
-        first = total.astype(BF16).astype(F32)
-        tile = jnp.where(lanes == 96, first, tile)
-        return jnp.where(lanes == 97, total - first, tile).astype(BF16)
-
-    for step in range(1, 4):
-        await_bytes(ra.at[step], r_ra + step)
+            rsend[row, col] = jnp.where(spots == 48, bias_term, turned[col * 32:(col + 1) * 32])
+        terms.append(remote(rsend.at[row], ra.at[x], device(g - x + row, p, c), slot(0), r_ra + x))
+        start_unless(x == row, terms[row])
+
+    def with_bias(tile, low_total, high_total):
+        lane_of = lax.broadcasted_iota(jnp.int32, tile.shape, 1)
+        bias_sum = jnp.where(lane_of < 64, low_total, high_total)
+        first = bias_sum.astype(BF16).astype(F32)
+        tile = jnp.where(lax.rem(lane_of, 64) == 48, first, tile)
+        return jnp.where(lax.rem(lane_of, 64) == 49, bias_sum - first, tile)
+
+    for step in range(1, 4):
+        from_x = mod4(x + step)
+        await_bytes(ra.at[from_x], r_ra + from_x)
+    xs = [mod4(x + step) for step in range(1, 4)]
+    halves = lax.broadcasted_iota(jnp.int32, (16, 128), 1) < 64
     for col in range(4):
-        summed = (rsend[x, col] + ra[1, col]) + (ra[2, col] + ra[3, col])
-        rbs[col] = with_bias(summed, summed[:, 96:97])
+        summed = (rsend[x, col] + ra[xs[0], col]) + (ra[xs[1], col] + ra[xs[2], col])
+        summed = with_bias(summed, summed[:, 48:49], summed[:, 48:49])
+        top, bottom = summed[0:16], summed[16:32]
+        rbs[col, 0] = jnp.where(halves, top, pltpu.roll(bottom, 64, 1)).astype(BF16)
+        rbs[col, 1] = jnp.where(halves, pltpu.roll(top, 64, 1), bottom).astype(BF16)
 
     r_rb = slot(1)
     to_group = zh * 4 + mod4(y + x)
     for step in range(1, 4):
         col = mod4(zh + step)
-        copy(rbs.at[col], rb.at[zl], device(to_group, x * 4 + col, c), r_rb)
-    r_zero = remote(rbs.at[zh], rb.at[zl], device(to_group, x * 4 + zh, c), slot(0), r_rb)
-
-    @pl.when(jnp.logical_not(stays))
-    def _():
-        r_zero.start()
+        for core in range(2):
+            copy(rbs.at[col, core], rb.at[zl, c], device(to_group, x * 4 + col, core), r_rb)
+    copy(rbs.at[zh, other], rb.at[zl, c], device(to_group, x * 4 + zh, other), r_rb)
+    r_zero = remote(rbs.at[zh, c], rb.at[zl, c], device(to_group, x * 4 + zh, c), slot(0), r_rb)
+    start_unless(stays, r_zero)
 
     @pl.when(stays)
     def _():
-        pltpu.make_async_copy(rbs.at[zh], rb.at[zl], recv_sem.at[r_rb]).start()
+        pltpu.make_async_copy(rbs.at[zh, c], rb.at[zl, c], recv_sem.at[r_rb]).start()
 
     await_bytes(rb, r_rb)
-    total = (rb[0].astype(F32) + rb[1].astype(F32)) + (rb[2].astype(F32) + rb[3].astype(F32))
-    fg[r_chip, c] = with_bias(total, total[:, 96:97] + total[:, 97:98])
+    for core in range(2):
+        total = (rb[0, core].astype(F32) + rb[1, core].astype(F32)) + (
+            rb[2, core].astype(F32) + rb[3, core].astype(F32)
+        )
+        fg[r_chip, core] = with_bias(
+            total, total[:, 48:49] + total[:, 49:50], total[:, 112:113] + total[:, 113:114]
+        ).astype(BF16)
 
     r_r2 = slot(1)
-    mine = fg.at[r_chip, c]
     for step in range(1, 16):
-        copy(mine, mine, device(lax.rem(g + step, 16), p, c), r_r2)
-    await_bytes(fg.at[pl.ds(0, 15), c], r_r2)
-    r_r3 = slot(1)
-    copy(fg.at[:, c], fg.at[:, c], partner, r_r3)
-    await_bytes(fg.at[:, other], r_r3)
+        copy(fg.at[r_chip], fg.at[r_chip], device(lax.rem(g + step, 16), p, c), r_r2)
+    await_bytes(fg.at[0:15], r_r2)
     for part in range(8):
-        rows = [fg[2 * part + j, core].astype(F32) for j in range(2) for core in range(2)]
-        fin[:, part * 128:(part + 1) * 128] = jnp.concatenate(rows, 0).T
-    out[32:56] = fin[pl.ds(pl.multiple_of(c * COLS, 8), COLS), :]
-    out[56:80] = fin[pl.ds(pl.multiple_of(PAIR + c * COLS, 8), COLS), :]
-    out[80:81] = fin[96:97, :] + fin[97:98, :]
+        rows = []
+        for chip in (2 * part, 2 * part + 1):
+            for core in range(2):
+                tile = fg[chip, core].astype(F32)
+                rows += [tile, pltpu.roll(tile, 64, 1)]
+        turned = jnp.concatenate(rows, 0).T
+        span = slice(part * 128, (part + 1) * 128)
+        gs_o[:, span] = turned[0:24]
+        gn_o[:, span] = turned[24:48]
+        gb_o[:, span] = turned[48:49] + turned[49:50]
 
     for made in sent:
         made.wait_send()
@@ -468,17 +495,31 @@
     def _():
         r_zero.wait_send()
 
+    for row in range(4):
+        @pl.when(x != row)
+        def _():
+            terms[row].wait_send()
+
     assert used[0] <= SENDS and used[1] <= RECVS, used
+
+
+OUTS = (
+    jax.ShapeDtypeStruct((32, 1024), BF16),
+    jax.ShapeDtypeStruct((COLS, 1024), F32),
+    jax.ShapeDtypeStruct((COLS, 1024), F32),
+    jax.ShapeDtypeStruct((1, 1024), F32),
+)
 
 
 def shards(features, adjacency, offsets, live, w_self, w_neigh, bias, targets):
     vmem = pl.BlockSpec(memory_space=pltpu.VMEM)
     hbm = pl.BlockSpec(memory_space=pltpu.HBM)
-    joined = pl.pallas_call(
+    inputs = [features.T, adjacency, offsets, live, w_self, w_neigh, bias.reshape(1, 1024), targets]
+    hidden, grad_self, grad_neigh, grad_bias = pl.pallas_call(
         kernel,
-        out_shape=jax.ShapeDtypeStruct((88, 1024), F32),
+        out_shape=OUTS,
         in_specs=[hbm] * 8,
-        out_specs=vmem,
+        out_specs=(vmem,) * 4,
         scratch_shapes=[
             pltpu.VMEM((COLS, 1024), BF16),
             pltpu.VMEM((8, TILE, 256), BF16),
@@ -499,22 +540,19 @@
             pltpu.VMEM((32, 1024), F32),
             pltpu.VMEM((4, 4, 32, 128), F32),
             pltpu.VMEM((4, 4, 32, 128), F32),
-            pltpu.VMEM((4, 32, 128), BF16),
-            pltpu.VMEM((4, 32, 128), BF16),
-            pltpu.VMEM((16, 2, 32, 128), BF16),
-            pltpu.VMEM((128, 1024), F32),
+            pltpu.VMEM((4, 2, 16, 128), BF16),
+            pltpu.VMEM((4, 2, 16, 128), BF16),
+            pltpu.VMEM((16, 2, 16, 128), BF16),
             pltpu.SemaphoreType.DMA((8,)),
             pltpu.SemaphoreType.DMA((SENDS,)),
             pltpu.SemaphoreType.DMA((RECVS,)),
         ],
         compiler_params=pltpu.CompilerParams(
-            collective_id=0, has_side_effects=True, vmem_limit_bytes=63 * 1024 * 1024
+            collective_id=0, has_side_effects=True, vmem_limit_bytes=48 * 1024 * 1024
         ),
         cost_estimate=pl.CostEstimate(flops=10**9, bytes_accessed=10**7, transcendentals=32768),
-    )(
-        features.T, adjacency, offsets, live, w_self, w_neigh, bias.reshape(1, 1024), targets
-    )
-    return joined[0:32].astype(BF16), joined[32:56], joined[56:80], joined[80]
+    )(*[pltpu.with_memory_space_constraint(array, pltpu.HBM) for array in inputs])
+    return hidden, grad_self, grad_neigh, grad_bias.reshape(1024)
 
 
 def solution(mesh):

time: 74.8 us -> 67.5 us (0.902)
  Pallas kernels: 69.4 us -> 64.2 us
  local copies, waits for them, and re-layouts: 4.52 us -> 2.51 us
    pallas_call x1, Pallas kernels: 69.4 us -> 64.2 us  [shards(): pl.pallas_call(kernel, out_shape=OUTS, in_specs=[hbm] * 8, out_specs=(vme...]
    slice x3 -> x0, local copies, waits for them, and re-layouts: 4.52 us -> none  [shards(): return (joined[0:32].astype(BF16), joined[32:56], joined[56:80], joined[80])]
    unnamed x0 -> x4, local copies, waits for them, and re-layouts: none -> 2.51 us
where the time goes in v2:
time: 67.5 us; the launch traced here: 67.3 us
  Pallas kernels  64.2 us (95%)
  local copies, waits for them, and re-layouts  2.51 us (4%)
    pallas_call x1, Pallas kernels, shards(): pl.pallas_call(kernel, out_shape=OUTS, in_specs=[hbm] * 8, out_specs=(vme...  64.2 us
    unnamed x4, local copies, waits for them, and re-layouts  2.51 us

profile of v2, /device:TPU:1, one launch (start us, length us, event | category | flops | bytes accessed | tf_op | source)
XLA Modules:
  0.0 67.3 jit_solution(109947935923232737)
XLA Ops:
  0.6 64.2 %shard_map.111 = (bf16[32,1024]{1,0:T(8,128)(2,1)S(1)}, f32[24,1024]{1,0:T(8,128)S(1)}, f32[24,1024]{1,0:T(8,128)S(1)}, f32[1,1024]{1,0:T(1,128)S(1)}) custom-call(bf16[24,1024]{1,0:T(8,128)(2,1)} %bitcast.4, bf16[8,128,256]{2,1,0:T(8,128)(2,1)} %adj_h.1, s32[8]{0:T(128)} %off_h.1, s32[8]{0:T(128)} %live_h.1, bf16[24,1024]{1,0:T(8,128)(2,1)} %ws_h.1, ...), custom_call_target="tpu_custom_call" | custom-call | flops 1000000000 | bytes 10000000 | tf_op jit(solution)/shard_map/pallas_call | solution.py:518
  64.8 0.6 copy.16
  65.5 0.6 copy.17
  66.1 0.6 copy.18
  66.7 0.6 copy.19

commit v3 on v2

--- a/solution.py
+++ b/solution.py
@@ -17,7 +17,7 @@
 PART_B = HALF - PART_A
 TILE = 128
 SENDS = 96
-RECVS = 64
+RECVS = 72
 
 
 def mod4(value):
@@ -227,7 +227,7 @@
 
     r_z1 = slot(1, 4)
     r_z2 = slot(1, 2)
-    r_y1 = slot(1, 6)
+    r_y1 = slot(1, 12)
     r_y2 = slot(1, 6)
     r_y3 = slot(1, 6)
 
@@ -253,17 +253,21 @@
     def column(number):
         return zh + sign * (0, -1, 1)[number]
 
-    def send_y1(number):
-        forward(y, column(number), "all", y_fwd, r_y1 + 2 * number)
-        forward(y, column(number), "all", y_bwd, r_y1 + 2 * number + 1)
+    def send_y1(number, part):
+        first = r_y1 + 4 * number + (0 if part == "a" else 2)
+        forward(y, column(number), part, y_fwd, first)
+        forward(y, column(number), part, y_bwd, first + 1)
 
     def take_y1(number):
         bz = column(number)
-        await_bytes(block(y - sign, bz, "all"), r_y1 + 2 * number)
+        first = r_y1 + 4 * number
+        await_bytes(block(y - sign, bz, "a"), first)
         forward(y - sign, bz, "a", y_fwd, r_y2 + 2 * number)
-        await_bytes(block(y + sign, bz, "all"), r_y1 + 2 * number + 1)
+        await_bytes(block(y + sign, bz, "b"), first + 3)
         forward(y + sign, bz, "b", y_bwd, r_y2 + 2 * number + 1)
+        await_bytes(block(y - sign, bz, "b"), first + 2)
         share(y - sign, bz, "all")
+        await_bytes(block(y + sign, bz, "a"), first + 1)
         share(y + sign, bz, "all")
 
     def take_y2(number):
@@ -286,7 +290,8 @@
             await_bytes(block(by, zh + 2, part), first + offset)
             share(by, zh + 2, part)
 
-    send_y1(0)
+    send_y1(0, "a")
+    send_y1(0, "b")
     share(y, zh, "all")
 
     for load in loads[3:6]:
@@ -319,14 +324,9 @@
 
     await_bytes(block(y, zh - sign, "a"), r_z1)
     forward(y, zh - sign, "a", z_fwd, r_z2)
-    await_bytes(block(y, zh + sign, "b"), r_z1 + 1)
-    forward(y, zh + sign, "b", z_bwd, r_z2 + 1)
+    send_y1(1, "a")
     await_bytes(block(y, zh + sign, "a"), r_z1 + 3)
-    send_y1(2)
-    await_bytes(block(y, zh - sign, "b"), r_z1 + 2)
-    send_y1(1)
-    share(y, zh - sign, "all")
-    share(y, zh + sign, "all")
+    send_y1(2, "a")
 
     await_bytes(wg.at[other], r_w3)
     for col in range(4):
@@ -362,8 +362,15 @@
         )
 
     compute(zh)
+    await_bytes(block(y, zh + sign, "b"), r_z1 + 1)
+    forward(y, zh + sign, "b", z_bwd, r_z2 + 1)
+    send_y1(2, "b")
+    await_bytes(block(y, zh - sign, "b"), r_z1 + 2)
+    send_y1(1, "b")
+    share(y, zh - sign, "all")
+    share(y, zh + sign, "all")
+    take_y1(1)
     take_y1(2)
-    take_y1(1)
     await_bytes(block(y, zh + 2, "a"), r_z2)
     send_y3("a")
     await_bytes(block(y, zh + 2, "b"), r_z2 + 1)
@@ -511,11 +518,20 @@
 )
 
 
+def place(hid, gs, gn, gb, hid_o, gs_o, gn_o, gb_o, sem):
+    pairs = [(hid, hid_o), (gs, gs_o), (gn, gn_o), (gb, gb_o)]
+    moves = [pltpu.make_async_copy(src, dst, sem.at[i]) for i, (src, dst) in enumerate(pairs)]
+    for move in moves:
+        move.start()
+    for move in moves:
+        move.wait()
+
+
 def shards(features, adjacency, offsets, live, w_self, w_neigh, bias, targets):
     vmem = pl.BlockSpec(memory_space=pltpu.VMEM)
     hbm = pl.BlockSpec(memory_space=pltpu.HBM)
     inputs = [features.T, adjacency, offsets, live, w_self, w_neigh, bias.reshape(1, 1024), targets]
-    hidden, grad_self, grad_neigh, grad_bias = pl.pallas_call(
+    results = pl.pallas_call(
         kernel,
         out_shape=OUTS,
         in_specs=[hbm] * 8,
@@ -552,6 +568,14 @@
         ),
         cost_estimate=pl.CostEstimate(flops=10**9, bytes_accessed=10**7, transcendentals=32768),
     )(*[pltpu.with_memory_space_constraint(array, pltpu.HBM) for array in inputs])
+    hidden, grad_self, grad_neigh, grad_bias = pl.pallas_call(
+        place,
+        out_shape=OUTS,
+        in_specs=[vmem] * 4,
+        out_specs=(pl.BlockSpec(memory_space=pl.ANY),) * 4,
+        scratch_shapes=[pltpu.SemaphoreType.DMA((4,))],
+        compiler_params=pltpu.CompilerParams(vmem_limit_bytes=1024 * 1024),
+    )(*[pltpu.with_memory_space_constraint(array, pltpu.VMEM) for array in results])
     return hidden, grad_self, grad_neigh, grad_bias.reshape(1024)
 
 

time: 67.5 us -> 67.5 us (level)
  local copies, waits for them, and re-layouts: 2.51 us -> 0 us
  Pallas kernels: 64.2 us -> 66.7 us
    unnamed x4 -> x0, local copies, waits for them, and re-layouts: 2.51 us -> none
    pallas_call x1, Pallas kernels: 64.2 us -> 66 us  [shards(): pl.pallas_call(kernel, out_shape=OUTS, in_specs=[hbm] * 8, out_specs=(vme...]
    pallas_call x0 -> x1, Pallas kernels: none -> 0.73 us  [shards(): pl.pallas_call(place, out_shape=OUTS, in_specs=[vmem] * 4, out_specs=(pl....]
where the time goes in v3:
time: 67.5 us; the launch traced here: 67.3 us
  Pallas kernels  66.7 us (99%)
    pallas_call x1, Pallas kernels, shards(): pl.pallas_call(kernel, out_shape=OUTS, in_specs=[hbm] * 8, out_specs=(vme...  66 us

profile of v3, /device:TPU:1, one launch (start us, length us, event | category | flops | bytes accessed | tf_op | source)
XLA Modules:
  0.0 67.3 jit_solution(4137016337261744895)
XLA Ops:
  0.6 66.0 %shard_map.111 = (bf16[32,1024]{1,0:T(8,128)(2,1)S(1)}, f32[24,1024]{1,0:T(8,128)S(1)}, f32[24,1024]{1,0:T(8,128)S(1)}, f32[1,1024]{1,0:T(1,128)S(1)}) custom-call(bf16[24,1024]{1,0:T(8,128)(2,1)} %bitcast.3, bf16[8,128,256]{2,1,0:T(8,128)(2,1)} %adj_h.1, s32[8]{0:T(128)} %off_h.1, s32[8]{0:T(128)} %live_h.1, bf16[24,1024]{1,0:T(8,128)(2,1)} %ws_h.1, ...), custom_call_target="tpu_custom_call" | custom-call | flops 1000000000 | bytes 10000000 | tf_op jit(solution)/shard_map/pallas_call | solution.py:534
  66.6 0.7 %shard_map.112 = (bf16[32,1024]{1,0:T(8,128)(2,1)}, f32[24,1024]{1,0:T(8,128)}, f32[24,1024]{1,0:T(8,128)}, f32[1,1024]{1,0:T(1,128)}) custom-call(bf16[32,1024]{1,0:T(8,128)(2,1)S(1)} %get-tuple-element.12.hid, f32[24,1024]{1,0:T(8,128)S(1)} %get-tuple-element.13.gs, f32[24,1024]{1,0:T(8,128)S(1)} %get-tuple-element.14.gn, f32[1,1024]{1,0:T(1,128)S(1)} %get-tuple-element.15.gb), custom_call_target="tpu_custom_call" | custom-call | tf_op jit(solution)/shard_map/pallas_call | solution.py:571

commit v4 on v3

--- a/solution.py
+++ b/solution.py
@@ -327,6 +327,13 @@
     send_y1(1, "a")
     await_bytes(block(y, zh + sign, "a"), r_z1 + 3)
     send_y1(2, "a")
+    await_bytes(block(y, zh + sign, "b"), r_z1 + 1)
+    forward(y, zh + sign, "b", z_bwd, r_z2 + 1)
+    send_y1(2, "b")
+    await_bytes(block(y, zh - sign, "b"), r_z1 + 2)
+    send_y1(1, "b")
+    share(y, zh - sign, "all")
+    share(y, zh + sign, "all")
 
     await_bytes(wg.at[other], r_w3)
     for col in range(4):
@@ -362,13 +369,6 @@
         )
 
     compute(zh)
-    await_bytes(block(y, zh + sign, "b"), r_z1 + 1)
-    forward(y, zh + sign, "b", z_bwd, r_z2 + 1)
-    send_y1(2, "b")
-    await_bytes(block(y, zh - sign, "b"), r_z1 + 2)
-    send_y1(1, "b")
-    share(y, zh - sign, "all")
-    share(y, zh + sign, "all")
     take_y1(1)
     take_y1(2)
     await_bytes(block(y, zh + 2, "a"), r_z2)
@@ -394,11 +394,16 @@
     rest = (delta - head.astype(F32)).astype(BF16)
     both = jnp.concatenate([head] * 4 + [rest] * 4, 0)
     turn = (((1,), (1,)), ((), ()))
-    lanes = lax.broadcasted_iota(jnp.int32, (32, 128), 1)
-    spots = lax.rem(lanes, 64)
     bias_term = jnp.sum(delta, axis=1, keepdims=True)
     quarter = lax.div(lax.broadcasted_iota(jnp.int32, (PAIR, 128), 1), 32)
     blank = jnp.zeros((16, 128), F32)
+
+    def with_bias(tile, low_total, high_total):
+        lane_of = lax.broadcasted_iota(jnp.int32, tile.shape, 1)
+        bias_sum = jnp.where(lane_of < 64, low_total, high_total)
+        first = bias_sum.astype(BF16).astype(F32)
+        tile = jnp.where(lax.rem(lane_of, 64) == 48, first, tile)
+        return jnp.where(lax.rem(lane_of, 64) == 49, bias_sum - first, tile)
 
     r_ra = slot(1, 4)
     terms = []
@@ -421,16 +426,10 @@
             [own_term[0:COLS], nb_term[0:COLS], blank, own_term[COLS:PAIR], nb_term[COLS:PAIR], blank], 0
         ).T
         for col in range(4):
-            rsend[row, col] = jnp.where(spots == 48, bias_term, turned[col * 32:(col + 1) * 32])
+            tile = with_bias(turned[col * 32:(col + 1) * 32], bias_term, bias_term)
+            rsend[row, col] = tile.astype(BF16)
         terms.append(remote(rsend.at[row], ra.at[x], device(g - x + row, p, c), slot(0), r_ra + x))
         start_unless(x == row, terms[row])
-
-    def with_bias(tile, low_total, high_total):
-        lane_of = lax.broadcasted_iota(jnp.int32, tile.shape, 1)
-        bias_sum = jnp.where(lane_of < 64, low_total, high_total)
-        first = bias_sum.astype(BF16).astype(F32)
-        tile = jnp.where(lax.rem(lane_of, 64) == 48, first, tile)
-        return jnp.where(lax.rem(lane_of, 64) == 49, bias_sum - first, tile)
 
     for step in range(1, 4):
         from_x = mod4(x + step)
@@ -438,8 +437,11 @@
     xs = [mod4(x + step) for step in range(1, 4)]
     halves = lax.broadcasted_iota(jnp.int32, (16, 128), 1) < 64
     for col in range(4):
-        summed = (rsend[x, col] + ra[xs[0], col]) + (ra[xs[1], col] + ra[xs[2], col])
-        summed = with_bias(summed, summed[:, 48:49], summed[:, 48:49])
+        summed = (rsend[x, col].astype(F32) + ra[xs[0], col].astype(F32)) + (
+            ra[xs[1], col].astype(F32) + ra[xs[2], col].astype(F32)
+        )
+        bias_sum = summed[:, 48:49] + summed[:, 49:50]
+        summed = with_bias(summed, bias_sum, bias_sum)
         top, bottom = summed[0:16], summed[16:32]
         rbs[col, 0] = jnp.where(halves, top, pltpu.roll(bottom, 64, 1)).astype(BF16)
         rbs[col, 1] = jnp.where(halves, pltpu.roll(top, 64, 1), bottom).astype(BF16)
@@ -554,8 +556,8 @@
             pltpu.VMEM((2, 16, 32, 128), BF16),
             pltpu.VMEM((4, 128, COLUMN), BF16),
             pltpu.VMEM((32, 1024), F32),
-            pltpu.VMEM((4, 4, 32, 128), F32),
-            pltpu.VMEM((4, 4, 32, 128), F32),
+            pltpu.VMEM((4, 4, 32, 128), BF16),
+            pltpu.VMEM((4, 4, 32, 128), BF16),
             pltpu.VMEM((4, 2, 16, 128), BF16),
             pltpu.VMEM((4, 2, 16, 128), BF16),
             pltpu.VMEM((16, 2, 16, 128), BF16),

time: 67.5 us -> 65.6 us (0.972)
  Pallas kernels: 66.7 us -> 64.8 us
    pallas_call x1, Pallas kernels: 66 us -> 64 us  [shards(): pl.pallas_call(kernel, out_shape=OUTS, in_specs=[hbm] * 8, out_specs=(vme...]
where the time goes in v4:
time: 65.6 us; the launch traced here: 65.4 us
  Pallas kernels  64.8 us (99%)
    pallas_call x1, Pallas kernels, shards(): pl.pallas_call(kernel, out_shape=OUTS, in_specs=[hbm] * 8, out_specs=(vme...  64 us

profile of v4, /device:TPU:1, one launch (start us, length us, event | category | flops | bytes accessed | tf_op | source)
XLA Modules:
  0.0 65.4 jit_solution(2014439101845948789)
XLA Ops:
  0.6 64.0 %shard_map.111 = (bf16[32,1024]{1,0:T(8,128)(2,1)S(1)}, f32[24,1024]{1,0:T(8,128)S(1)}, f32[24,1024]{1,0:T(8,128)S(1)}, f32[1,1024]{1,0:T(1,128)S(1)}) custom-call(bf16[24,1024]{1,0:T(8,128)(2,1)} %bitcast.3, bf16[8,128,256]{2,1,0:T(8,128)(2,1)} %adj_h.1, s32[8]{0:T(128)} %off_h.1, s32[8]{0:T(128)} %live_h.1, bf16[24,1024]{1,0:T(8,128)(2,1)} %ws_h.1, ...), custom_call_target="tpu_custom_call" | custom-call | flops 1000000000 | bytes 10000000 | tf_op jit(solution)/shard_map/pallas_call | solution.py:536
  64.7 0.7 %shard_map.112 = (bf16[32,1024]{1,0:T(8,128)(2,1)}, f32[24,1024]{1,0:T(8,128)}, f32[24,1024]{1,0:T(8,128)}, f32[1,1024]{1,0:T(1,128)}) custom-call(bf16[32,1024]{1,0:T(8,128)(2,1)S(1)} %get-tuple-element.12.hid, f32[24,1024]{1,0:T(8,128)S(1)} %get-tuple-element.13.gs, f32[24,1024]{1,0:T(8,128)S(1)} %get-tuple-element.14.gn, f32[1,1024]{1,0:T(1,128)S(1)} %get-tuple-element.15.gb), custom_call_target="tpu_custom_call" | custom-call | tf_op jit(solution)/shard_map/pallas_call | solution.py:573

commit v5 on v4

--- a/solution.py
+++ b/solution.py
@@ -302,31 +302,47 @@
         moved = pltpu.roll(padded, off[tile] - tile * TILE, 1)
         band[tile] = (moved * live[tile].astype(F32)).astype(BF16)
 
-    for step in range(1, 4):
-        await_bytes(wg.at[c, w_src_y * 4 + mod4(zh + step)], r_w1 + 4 - step)
-
-    @pl.when(x != 0)
-    def _():
-        await_bytes(wg.at[c, w_src_y * 4 + zh], r_w1)
-
-    r_w2 = slot(1, 4)
-    part_w = wg.at[c, pl.ds(w_src_y * 4, 4)]
-    for step in range(1, 4):
-        copy(part_w, part_w, device(g - x + mod4(x + step), p, c), r_w2 + step)
+    def neighbours(bz):
+        col = mod4(bz)
+        rows = pl.ds(pl.multiple_of(col * COLUMN, 16), COLUMN)
+        await_bytes(xg.at[rows, pl.ds(pl.multiple_of(other * HALF, 128), HALF)], r_pair + col)
+        for tile in range(8):
+            nb[rows, tile * TILE:(tile + 1) * TILE] = lax.dot_general(
+                xg[rows, tile * TILE:tile * TILE + 3 * TILE], band[tile],
+                (((1,), (1,)), ((), ())), preferred_element_type=F32,
+            ).astype(BF16)
+
+    def products(bz):
+        col = mod4(bz)
+        rows = pl.ds(pl.multiple_of(col * COLUMN, 16), COLUMN)
+        ws_t = wt[col, pl.ds(pl.multiple_of(c * 32, 16), 32), :]
+        wn_t = wt[col, pl.ds(pl.multiple_of(64 + c * 32, 16), 32), :]
+        pre_acc[...] += (
+            jnp.dot(ws_t, xg[rows, TILE:TILE + 1024], preferred_element_type=F32)
+            + jnp.dot(wn_t, nb[rows, :], preferred_element_type=F32)
+        )
 
     take_y1(0)
-
-    for step in range(1, 4):
-        await_bytes(wg.at[c, pl.ds(mod4(y + x - step) * 4, 4)], r_w2 + step)
-    r_w3 = slot(1)
-    copy(wg.at[c], wg.at[c], partner, r_w3)
-    take_y2(0)
 
     await_bytes(block(y, zh - sign, "a"), r_z1)
     forward(y, zh - sign, "a", z_fwd, r_z2)
     send_y1(1, "a")
     await_bytes(block(y, zh + sign, "a"), r_z1 + 3)
     send_y1(2, "a")
+
+    for step in range(1, 4):
+        await_bytes(wg.at[c, w_src_y * 4 + mod4(zh + step)], r_w1 + 4 - step)
+
+    @pl.when(x != 0)
+    def _():
+        await_bytes(wg.at[c, w_src_y * 4 + zh], r_w1)
+
+    r_w2 = slot(1, 4)
+    part_w = wg.at[c, pl.ds(w_src_y * 4, 4)]
+    for step in range(1, 4):
+        copy(part_w, part_w, device(g - x + mod4(x + step), p, c), r_w2 + step)
+
+    take_y2(0)
     await_bytes(block(y, zh + sign, "b"), r_z1 + 1)
     forward(y, zh + sign, "b", z_bwd, r_z2 + 1)
     send_y1(2, "b")
@@ -334,6 +350,19 @@
     send_y1(1, "b")
     share(y, zh - sign, "all")
     share(y, zh + sign, "all")
+    neighbours(zh)
+    for step in range(1, 4):
+        await_bytes(wg.at[c, pl.ds(mod4(y + x - step) * 4, 4)], r_w2 + step)
+    r_w3 = slot(1)
+    copy(wg.at[c], wg.at[c], partner, r_w3)
+    take_y1(1)
+    take_y1(2)
+    await_bytes(block(y, zh + 2, "a"), r_z2)
+    send_y3("a")
+    await_bytes(block(y, zh + 2, "b"), r_z2 + 1)
+    send_y3("b")
+    take_y2(2)
+    take_y2(1)
 
     await_bytes(wg.at[other], r_w3)
     for col in range(4):
@@ -342,7 +371,6 @@
             for core in range(2):
                 rows.append(wg[core, row * 4 + col].astype(F32)[0:COLS])
         wt[col] = jnp.concatenate(rows, 0).T.astype(BF16)
-
     loads[6].wait()
     spot = lax.broadcasted_iota(jnp.int32, (32, 1024), 1)
     row = lax.broadcasted_iota(jnp.int32, (32, 1024), 0)
@@ -351,37 +379,15 @@
         axis=1, keepdims=True,
     )
     pre_acc[...] = jnp.broadcast_to(bias_own, (32, 1024))
-
-    def compute(bz):
-        col = mod4(bz)
-        rows = pl.ds(pl.multiple_of(col * COLUMN, 16), COLUMN)
-        await_bytes(xg.at[rows, pl.ds(pl.multiple_of(other * HALF, 128), HALF)], r_pair + col)
-        for tile in range(8):
-            nb[rows, tile * TILE:(tile + 1) * TILE] = lax.dot_general(
-                xg[rows, tile * TILE:tile * TILE + 3 * TILE], band[tile],
-                (((1,), (1,)), ((), ())), preferred_element_type=F32,
-            ).astype(BF16)
-        ws_t = wt[col, pl.ds(pl.multiple_of(c * 32, 16), 32), :]
-        wn_t = wt[col, pl.ds(pl.multiple_of(64 + c * 32, 16), 32), :]
-        pre_acc[...] += (
-            jnp.dot(ws_t, xg[rows, TILE:TILE + 1024], preferred_element_type=F32)
-            + jnp.dot(wn_t, nb[rows, :], preferred_element_type=F32)
-        )
-
-    compute(zh)
-    take_y1(1)
-    take_y1(2)
-    await_bytes(block(y, zh + 2, "a"), r_z2)
-    send_y3("a")
-    await_bytes(block(y, zh + 2, "b"), r_z2 + 1)
-    send_y3("b")
-    take_y2(2)
-    take_y2(1)
-    compute(zh - 1)
-    compute(zh + 1)
+    products(zh)
+    neighbours(zh - 1)
+    neighbours(zh + 1)
+    products(zh - 1)
+    products(zh + 1)
     take_y3("a")
     take_y3("b")
-    compute(zh + 2)
+    neighbours(zh + 2)
+    products(zh + 2)
 
     loads[7].wait()
     pre = pre_acc[...]

time: 65.6 us -> 63.4 us (0.966)
  Pallas kernels: 64.8 us -> 62.6 us
    pallas_call x1, Pallas kernels: 64 us -> 61.9 us  [shards(): pl.pallas_call(kernel, out_shape=OUTS, in_specs=[hbm] * 8, out_specs=(vme...]
where the time goes in v5:
time: 63.4 us; the launch traced here: 63.3 us
  Pallas kernels  62.6 us (99%)
  between operations  0.64 us (1%)
    pallas_call x1, Pallas kernels, shards(): pl.pallas_call(kernel, out_shape=OUTS, in_specs=[hbm] * 8, out_specs=(vme...  61.9 us

profile of v5, /device:TPU:1, one launch (start us, length us, event | category | flops | bytes accessed | tf_op | source)
XLA Modules:
  0.0 63.3 jit_solution(7990202462851893539)
XLA Ops:
  0.6 61.9 %shard_map.111 = (bf16[32,1024]{1,0:T(8,128)(2,1)S(1)}, f32[24,1024]{1,0:T(8,128)S(1)}, f32[24,1024]{1,0:T(8,128)S(1)}, f32[1,1024]{1,0:T(1,128)S(1)}) custom-call(bf16[24,1024]{1,0:T(8,128)(2,1)} %bitcast.3, bf16[8,128,256]{2,1,0:T(8,128)(2,1)} %adj_h.1, s32[8]{0:T(128)} %off_h.1, s32[8]{0:T(128)} %live_h.1, bf16[24,1024]{1,0:T(8,128)(2,1)} %ws_h.1, ...), custom_call_target="tpu_custom_call" | custom-call | flops 1000000000 | bytes 10000000 | tf_op jit(solution)/shard_map/pallas_call | solution.py:542
  62.5 0.7 %shard_map.112 = (bf16[32,1024]{1,0:T(8,128)(2,1)}, f32[24,1024]{1,0:T(8,128)}, f32[24,1024]{1,0:T(8,128)}, f32[1,1024]{1,0:T(1,128)}) custom-call(bf16[32,1024]{1,0:T(8,128)(2,1)S(1)} %get-tuple-element.12.hid, f32[24,1024]{1,0:T(8,128)S(1)} %get-tuple-element.13.gs, f32[24,1024]{1,0:T(8,128)S(1)} %get-tuple-element.14.gn, f32[1,1024]{1,0:T(1,128)S(1)} %get-tuple-element.15.gb), custom_call_target="tpu_custom_call" | custom-call | tf_op jit(solution)/shard_map/pallas_call | solution.py:579

commit v6 on v5

--- a/solution.py
+++ b/solution.py
@@ -231,25 +231,6 @@
     r_y2 = slot(1, 6)
     r_y3 = slot(1, 6)
 
-    await_bytes(stage.at[other_rows, pl.ds(pl.multiple_of(other * TILE, 128), 512)], r_swap)
-    block(y, zh, "a")[...] = stage[:, pl.ds(pl.multiple_of(other * PART_B, 128), PART_A)].astype(BF16)
-    forward(y, zh, "a", z_fwd, r_z1)
-    forward(y, zh, "a", z_bwd, r_z1 + 3)
-
-    @pl.when(jnp.logical_and(c == 0, g > 0))
-    def _():
-        await_bytes(stage.at[0:COLS, 0:TILE], r_left)
-        await_bytes(stage.at[COLS:PAIR, 0:TILE], r_left + 1)
-
-    @pl.when(jnp.logical_and(c == 1, g < 15))
-    def _():
-        await_bytes(stage.at[0:COLS, 512:HALF], r_right)
-        await_bytes(stage.at[COLS:PAIR, 512:HALF], r_right + 1)
-
-    block(y, zh, "b")[...] = stage[:, pl.ds(pl.multiple_of(c * PART_A, 128), PART_B)].astype(BF16)
-    forward(y, zh, "b", z_bwd, r_z1 + 1)
-    forward(y, zh, "b", z_fwd, r_z1 + 2)
-
     def column(number):
         return zh + sign * (0, -1, 1)[number]
 
@@ -290,7 +271,26 @@
             await_bytes(block(by, zh + 2, part), first + offset)
             share(by, zh + 2, part)
 
+    await_bytes(stage.at[other_rows, pl.ds(pl.multiple_of(other * TILE, 128), 512)], r_swap)
+    block(y, zh, "a")[...] = stage[:, pl.ds(pl.multiple_of(other * PART_B, 128), PART_A)].astype(BF16)
+    forward(y, zh, "a", z_fwd, r_z1)
+    forward(y, zh, "a", z_bwd, r_z1 + 3)
     send_y1(0, "a")
+
+    @pl.when(jnp.logical_and(c == 0, g > 0))
+    def _():
+        await_bytes(stage.at[0:COLS, 0:TILE], r_left)
+        await_bytes(stage.at[COLS:PAIR, 0:TILE], r_left + 1)
+
+    @pl.when(jnp.logical_and(c == 1, g < 15))
+    def _():
+        await_bytes(stage.at[0:COLS, 512:HALF], r_right)
+        await_bytes(stage.at[COLS:PAIR, 512:HALF], r_right + 1)
+
+    block(y, zh, "b")[...] = stage[:, pl.ds(pl.multiple_of(c * PART_A, 128), PART_B)].astype(BF16)
+    forward(y, zh, "b", z_bwd, r_z1 + 1)
+    forward(y, zh, "b", z_fwd, r_z1 + 2)
+
     send_y1(0, "b")
     share(y, zh, "all")
 
@@ -412,9 +412,11 @@
         return jnp.where(lax.rem(lane_of, 64) == 49, bias_sum - first, tile)
 
     r_ra = slot(1, 4)
-    terms = []
-    for row in range(4):
-        spans = [slice((col * 4 + row) * PAIR, (col * 4 + row + 1) * PAIR) for col in range(4)]
+    for turn_of in range(1, 5):
+        row = mod4(x + turn_of)
+        spans = [
+            pl.ds(pl.multiple_of((col * 4 + row) * PAIR, 16), PAIR) for col in range(4)
+        ]
         left = jnp.concatenate(
             [xg[span, TILE:TILE + 1024] for span in spans] + [nb[span, :] for span in spans], 0
         )
@@ -434,30 +436,29 @@
         for col in range(4):
             tile = with_bias(turned[col * 32:(col + 1) * 32], bias_term, bias_term)
             rsend[row, col] = tile.astype(BF16)
-        terms.append(remote(rsend.at[row], ra.at[x], device(g - x + row, p, c), slot(0), r_ra + x))
-        start_unless(x == row, terms[row])
-
-    for step in range(1, 4):
-        from_x = mod4(x + step)
-        await_bytes(ra.at[from_x], r_ra + from_x)
-    xs = [mod4(x + step) for step in range(1, 4)]
+        if turn_of < 4:
+            copy(rsend.at[row], ra.at[turn_of], device(g - x + row, p, c), r_ra + turn_of)
+
+    for turn_of in range(1, 4):
+        await_bytes(ra.at[turn_of], r_ra + turn_of)
+
+    r_rb = slot(1)
+    to_group = zh * 4 + mod4(y + x)
     halves = lax.broadcasted_iota(jnp.int32, (16, 128), 1) < 64
-    for col in range(4):
-        summed = (rsend[x, col].astype(F32) + ra[xs[0], col].astype(F32)) + (
-            ra[xs[1], col].astype(F32) + ra[xs[2], col].astype(F32)
+    for step in (2, 1, 3, 0):
+        col = mod4(zh + step)
+        summed = (rsend[x, col].astype(F32) + ra[1, col].astype(F32)) + (
+            ra[2, col].astype(F32) + ra[3, col].astype(F32)
         )
         bias_sum = summed[:, 48:49] + summed[:, 49:50]
         summed = with_bias(summed, bias_sum, bias_sum)
         top, bottom = summed[0:16], summed[16:32]
         rbs[col, 0] = jnp.where(halves, top, pltpu.roll(bottom, 64, 1)).astype(BF16)
         rbs[col, 1] = jnp.where(halves, pltpu.roll(top, 64, 1), bottom).astype(BF16)
-
-    r_rb = slot(1)
-    to_group = zh * 4 + mod4(y + x)
-    for step in range(1, 4):
-        col = mod4(zh + step)
-        for core in range(2):
-            copy(rbs.at[col, core], rb.at[zl, c], device(to_group, x * 4 + col, core), r_rb)
+        if step:
+            for core in range(2):
+                copy(rbs.at[col, core], rb.at[zl, c], device(to_group, x * 4 + col, core), r_rb)
+
     copy(rbs.at[zh, other], rb.at[zl, c], device(to_group, x * 4 + zh, other), r_rb)
     r_zero = remote(rbs.at[zh, c], rb.at[zl, c], device(to_group, x * 4 + zh, c), slot(0), r_rb)
     start_unless(stays, r_zero)
@@ -475,21 +476,24 @@
             total, total[:, 48:49] + total[:, 49:50], total[:, 112:113] + total[:, 113:114]
         ).astype(BF16)
 
-    r_r2 = slot(1)
+    r_r2 = slot(1, 4)
     for step in range(1, 16):
-        copy(fg.at[r_chip], fg.at[r_chip], device(lax.rem(g + step, 16), p, c), r_r2)
-    await_bytes(fg.at[0:15], r_r2)
-    for part in range(8):
-        rows = []
-        for chip in (2 * part, 2 * part + 1):
-            for core in range(2):
-                tile = fg[chip, core].astype(F32)
-                rows += [tile, pltpu.roll(tile, 64, 1)]
-        turned = jnp.concatenate(rows, 0).T
-        span = slice(part * 128, (part + 1) * 128)
-        gs_o[:, span] = turned[0:24]
-        gn_o[:, span] = turned[24:48]
-        gb_o[:, span] = turned[48:49] + turned[49:50]
+        far = lax.rem(g + step, 16)
+        copy(fg.at[r_chip], fg.at[r_chip], device(far, p, c), r_r2 + mod4(x - lax.rem(far, 4)))
+    for k in (0, 1, 3, 2):
+        await_bytes(fg.at[0:(4 if k else 3)], r_r2 + k)
+        for half in range(2):
+            part = lax.rem(x - y + k + 4, 4) * 2 + half
+            rows = []
+            for chip in range(2):
+                for core in range(2):
+                    tile = fg[2 * part + chip, core].astype(F32)
+                    rows += [tile, pltpu.roll(tile, 64, 1)]
+            turned = jnp.concatenate(rows, 0).T
+            span = pl.ds(pl.multiple_of(part * 128, 128), 128)
+            gs_o[:, span] = turned[0:24]
+            gn_o[:, span] = turned[24:48]
+            gb_o[:, span] = turned[48:49] + turned[49:50]
 
     for made in sent:
         made.wait_send()
@@ -509,11 +513,6 @@
     @pl.when(jnp.logical_not(stays))
     def _():
         r_zero.wait_send()
-
-    for row in range(4):
-        @pl.when(x != row)
-        def _():
-            terms[row].wait_send()
 
     assert used[0] <= SENDS and used[1] <= RECVS, used
 

time: 63.4 us -> 63.5 us (level)
  no operation moved by 1% of the time
where the time goes in v6:
time: 63.5 us; the launch traced here: 63.4 us
  Pallas kernels  62.7 us (99%)
  between operations  0.64 us (1%)
    pallas_call x1, Pallas kernels, shards(): pl.pallas_call(kernel, out_shape=OUTS, in_specs=[hbm] * 8, out_specs=(vme...  62 us

profile of v6, /device:TPU:1, one launch (start us, length us, event | category | flops | bytes accessed | tf_op | source)
XLA Modules:
  0.0 63.4 jit_solution(16646123448075974133)
XLA Ops:
  0.6 62.0 %shard_map.111 = (bf16[32,1024]{1,0:T(8,128)(2,1)S(1)}, f32[24,1024]{1,0:T(8,128)S(1)}, f32[24,1024]{1,0:T(8,128)S(1)}, f32[1,1024]{1,0:T(1,128)S(1)}) custom-call(bf16[24,1024]{1,0:T(8,128)(2,1)} %bitcast.3, bf16[8,128,256]{2,1,0:T(8,128)(2,1)} %adj_h.1, s32[8]{0:T(128)} %off_h.1, s32[8]{0:T(128)} %live_h.1, bf16[24,1024]{1,0:T(8,128)(2,1)} %ws_h.1, ...), custom_call_target="tpu_custom_call" | custom-call | flops 1000000000 | bytes 10000000 | tf_op jit(solution)/shard_map/pallas_call | solution.py:541
  62.6 0.7 %shard_map.112 = (bf16[32,1024]{1,0:T(8,128)(2,1)}, f32[24,1024]{1,0:T(8,128)}, f32[24,1024]{1,0:T(8,128)}, f32[1,1024]{1,0:T(1,128)}) custom-call(bf16[32,1024]{1,0:T(8,128)(2,1)S(1)} %get-tuple-element.12.hid, f32[24,1024]{1,0:T(8,128)S(1)} %get-tuple-element.13.gs, f32[24,1024]{1,0:T(8,128)S(1)} %get-tuple-element.14.gn, f32[1,1024]{1,0:T(1,128)S(1)} %get-tuple-element.15.gb), custom_call_target="tpu_custom_call" | custom-call | tf_op jit(solution)/shard_map/pallas_call | solution.py:578

commit v7 on v6

--- a/solution.py
+++ b/solution.py
@@ -28,7 +28,7 @@
     feat_h, adj_h, off_h, live_h, ws_h, wn_h, bias_h, tgt_h,
     hid, gs_o, gn_o, gb_o,
     feat, adj, off, live, ws, wn, bias, tgt,
-    wide, stage, xg, nb, band, wsend, wg, wt, pre_acc, rsend, ra, rbs, rb, fg,
+    wide, edge, xr, xg, nb, band, wsend, wg, wt, pre_acc, rsend, ra, rbs, rb, fg,
     in_sem, send_sem, recv_sem,
 ):
     loads = [
@@ -68,16 +68,6 @@
     def tell(target):
         pl.semaphore_signal(barrier, inc=1, device_id=target, device_id_type=MESH)
 
-    @pl.when(jnp.logical_and(c == 0, g > 0))
-    def _():
-        tell(device(g - 1, p, 0))
-        tell(device(g - 1, p, 1))
-
-    @pl.when(jnp.logical_and(c == 1, g < 15))
-    def _():
-        tell(device(g + 1, p, 0))
-        tell(device(g + 1, p, 1))
-
     for target in (z_fwd, z_bwd, y_fwd, y_bwd, y_far, partner):
         tell(target)
 
@@ -108,28 +98,22 @@
     loads[0].wait()
     wide[...] = feat[...].astype(F32)
 
-    @pl.when(c == 0)
-    def _():
-        stage[0:COLS, TILE:HALF] = wide[:, 0:512]
-
-        @pl.when(g == 0)
-        def _():
-            stage[:, 0:TILE] = jnp.zeros((PAIR, TILE), F32)
-
-    @pl.when(c == 1)
-    def _():
-        stage[COLS:PAIR, 0:512] = wide[:, 512:1024]
-
-        @pl.when(g == 15)
-        def _():
-            stage[:, 512:HALF] = jnp.zeros((PAIR, TILE), F32)
+    own_row = ((zh * 2 + c) * 4 + y) * PAIR
+    own = pl.ds(pl.multiple_of(own_row, 16), PAIR)
+    xr[own, 0:512] = jnp.concatenate([wide[:, 0:512], wide[:, 512:1024]], 0).astype(BF16)
+
+    @pl.when(g == 0)
+    def _():
+        edge[0:COLS] = jnp.zeros((COLS, TILE), F32)
+
+    @pl.when(g == 15)
+    def _():
+        edge[COLS:PAIR] = jnp.zeros((COLS, TILE), F32)
 
     waits = (
         6 + 3 + 7 + 15
         + (x != 0).astype(jnp.int32)
         + jnp.logical_not(stays).astype(jnp.int32)
-        + (g < 15).astype(jnp.int32)
-        + (g > 0).astype(jnp.int32)
     )
     pl.semaphore_wait(barrier, waits)
 
@@ -159,14 +143,12 @@
     def await_bytes(ref, recv):
         pltpu.make_async_copy(ref, ref, recv_sem.at[recv]).wait()
 
-    own_rows = pl.ds(pl.multiple_of(c * COLS, 8), COLS)
-    other_rows = pl.ds(pl.multiple_of(other * COLS, 8), COLS)
-    r_left, r_right, r_swap = slot(1, 2), slot(1, 2), slot(1)
+    r_left, r_right = slot(1), slot(1)
     halo_up = remote(
-        wide.at[:, 896:1024], stage.at[own_rows, 0:TILE], device(g + 1, p, 0), slot(0), r_left + c
+        wide.at[:, 896:1024], edge.at[0:COLS], device(g + 1, p, c), slot(0), r_left
     )
     halo_down = remote(
-        wide.at[:, 0:TILE], stage.at[own_rows, 512:HALF], device(g - 1, p, 1), slot(0), r_right + c
+        wide.at[:, 0:TILE], edge.at[COLS:PAIR], device(g - 1, p, c), slot(0), r_right
     )
 
     @pl.when(g < 15)
@@ -177,11 +159,70 @@
     def _():
         halo_down.start()
 
-    copy(
-        wide.at[:, pl.ds(pl.multiple_of(other * 512, 128), 512)],
-        stage.at[own_rows, pl.ds(pl.multiple_of(c * TILE, 128), 512)],
-        partner, r_swap,
-    )
+    def block(by, bz, part):
+        first = (mod4(bz) * 2 + c) * 4 + mod4(by)
+        start = {"all": 0, "a": 0, "b": PART_A}[part]
+        width = {"all": HALF, "a": PART_A, "b": PART_B}[part]
+        return xr.at[pl.ds(pl.multiple_of(first * PAIR, 16), PAIR), start:start + width]
+
+    r_pair = slot(1, 4)
+
+    def forward(by, bz, part, target, recv):
+        view = block(by, bz, part)
+        copy(view, view, target, recv)
+
+    def share(by, bz, part):
+        forward(by, bz, part, partner, r_pair + mod4(bz))
+
+    r_z1 = slot(1, 4)
+    r_z2 = slot(1, 2)
+    r_y1 = slot(1, 12)
+    r_y2 = slot(1, 6)
+    r_y3 = slot(1, 6)
+
+    def column(number):
+        return zh + sign * (0, -1, 1)[number]
+
+    def send_y1(number, part):
+        first = r_y1 + 4 * number + (0 if part == "a" else 2)
+        forward(y, column(number), part, y_fwd, first)
+        forward(y, column(number), part, y_bwd, first + 1)
+
+    def take_y1(number):
+        bz = column(number)
+        first = r_y1 + 4 * number
+        await_bytes(block(y - sign, bz, "a"), first)
+        forward(y - sign, bz, "a", y_fwd, r_y2 + 2 * number)
+        await_bytes(block(y + sign, bz, "b"), first + 3)
+        forward(y + sign, bz, "b", y_bwd, r_y2 + 2 * number + 1)
+        await_bytes(block(y - sign, bz, "b"), first + 2)
+        share(y - sign, bz, "all")
+        await_bytes(block(y + sign, bz, "a"), first + 1)
+        share(y + sign, bz, "all")
+
+    def take_y2(number):
+        bz = column(number)
+        await_bytes(block(y + 2, bz, "a"), r_y2 + 2 * number)
+        share(y + 2, bz, "a")
+        await_bytes(block(y + 2, bz, "b"), r_y2 + 2 * number + 1)
+        share(y + 2, bz, "b")
+
+    def send_y3(part):
+        first = r_y3 + (0 if part == "a" else 3)
+        forward(y, zh + 2, part, y_fwd, first)
+        forward(y, zh + 2, part, y_bwd, first + 1)
+        forward(y, zh + 2, part, y_far, first + 2)
+        share(y, zh + 2, part)
+
+    def take_y3(part):
+        first = r_y3 + (0 if part == "a" else 3)
+        for offset, by in enumerate((y - sign, y + sign, y + 2)):
+            await_bytes(block(by, zh + 2, part), first + offset)
+            share(by, zh + 2, part)
+
+    forward(y, zh, "a", z_fwd, r_z1)
+    forward(y, zh, "a", z_bwd, r_z1 + 3)
+    send_y1(0, "a")
 
     loads[1].wait()
     loads[2].wait()
@@ -210,84 +251,15 @@
     def _():
         wg[c, p] = wsend[chip0]
 
-    def block(by, bz, part):
-        rows = pl.ds(pl.multiple_of((mod4(bz) * 4 + mod4(by)) * PAIR, 16), PAIR)
-        start = {"all": 0, "a": other * PART_B, "b": c * PART_A}[part]
-        width = {"all": HALF, "a": PART_A, "b": PART_B}[part]
-        return xg.at[rows, pl.ds(pl.multiple_of(c * HALF + start, 128), width)]
-
-    r_pair = slot(1, 4)
-
-    def forward(by, bz, part, target, recv):
-        view = block(by, bz, part)
-        copy(view, view, target, recv)
-
-    def share(by, bz, part):
-        forward(by, bz, part, partner, r_pair + mod4(bz))
-
-    r_z1 = slot(1, 4)
-    r_z2 = slot(1, 2)
-    r_y1 = slot(1, 12)
-    r_y2 = slot(1, 6)
-    r_y3 = slot(1, 6)
-
-    def column(number):
-        return zh + sign * (0, -1, 1)[number]
-
-    def send_y1(number, part):
-        first = r_y1 + 4 * number + (0 if part == "a" else 2)
-        forward(y, column(number), part, y_fwd, first)
-        forward(y, column(number), part, y_bwd, first + 1)
-
-    def take_y1(number):
-        bz = column(number)
-        first = r_y1 + 4 * number
-        await_bytes(block(y - sign, bz, "a"), first)
-        forward(y - sign, bz, "a", y_fwd, r_y2 + 2 * number)
-        await_bytes(block(y + sign, bz, "b"), first + 3)
-        forward(y + sign, bz, "b", y_bwd, r_y2 + 2 * number + 1)
-        await_bytes(block(y - sign, bz, "b"), first + 2)
-        share(y - sign, bz, "all")
-        await_bytes(block(y + sign, bz, "a"), first + 1)
-        share(y + sign, bz, "all")
-
-    def take_y2(number):
-        bz = column(number)
-        await_bytes(block(y + 2, bz, "a"), r_y2 + 2 * number)
-        share(y + 2, bz, "a")
-        await_bytes(block(y + 2, bz, "b"), r_y2 + 2 * number + 1)
-        share(y + 2, bz, "b")
-
-    def send_y3(part):
-        first = r_y3 + (0 if part == "a" else 3)
-        forward(y, zh + 2, part, y_fwd, first)
-        forward(y, zh + 2, part, y_bwd, first + 1)
-        forward(y, zh + 2, part, y_far, first + 2)
-        share(y, zh + 2, part)
-
-    def take_y3(part):
-        first = r_y3 + (0 if part == "a" else 3)
-        for offset, by in enumerate((y - sign, y + sign, y + 2)):
-            await_bytes(block(by, zh + 2, part), first + offset)
-            share(by, zh + 2, part)
-
-    await_bytes(stage.at[other_rows, pl.ds(pl.multiple_of(other * TILE, 128), 512)], r_swap)
-    block(y, zh, "a")[...] = stage[:, pl.ds(pl.multiple_of(other * PART_B, 128), PART_A)].astype(BF16)
-    forward(y, zh, "a", z_fwd, r_z1)
-    forward(y, zh, "a", z_bwd, r_z1 + 3)
-    send_y1(0, "a")
-
-    @pl.when(jnp.logical_and(c == 0, g > 0))
-    def _():
-        await_bytes(stage.at[0:COLS, 0:TILE], r_left)
-        await_bytes(stage.at[COLS:PAIR, 0:TILE], r_left + 1)
-
-    @pl.when(jnp.logical_and(c == 1, g < 15))
-    def _():
-        await_bytes(stage.at[0:COLS, 512:HALF], r_right)
-        await_bytes(stage.at[COLS:PAIR, 512:HALF], r_right + 1)
-
-    block(y, zh, "b")[...] = stage[:, pl.ds(pl.multiple_of(c * PART_A, 128), PART_B)].astype(BF16)
+    @pl.when(g > 0)
+    def _():
+        await_bytes(edge.at[0:COLS], r_left)
+
+    @pl.when(g < 15)
+    def _():
+        await_bytes(edge.at[COLS:PAIR], r_right)
+
+    xr[own, 512:HALF] = edge[...].astype(BF16)
     forward(y, zh, "b", z_bwd, r_z1 + 1)
     forward(y, zh, "b", z_fwd, r_z1 + 2)
 
@@ -305,7 +277,20 @@
     def neighbours(bz):
         col = mod4(bz)
         rows = pl.ds(pl.multiple_of(col * COLUMN, 16), COLUMN)
-        await_bytes(xg.at[rows, pl.ds(pl.multiple_of(other * HALF, 128), HALF)], r_pair + col)
+        theirs = pl.ds(pl.multiple_of((col * 2 + other) * COLUMN, 16), COLUMN)
+        await_bytes(xr.at[theirs], r_pair + col)
+        for row in range(4):
+            cores = []
+            for core in range(2):
+                first = ((col * 2 + core) * 4 + row) * PAIR
+                cores.append(xr[pl.ds(pl.multiple_of(first, 16), PAIR), :].astype(F32))
+            low = jnp.concatenate([half[0:COLS] for half in cores], 0).astype(BF16)
+            high = jnp.concatenate([half[COLS:PAIR] for half in cores], 0).astype(BF16)
+            here = pl.ds(pl.multiple_of((col * 4 + row) * PAIR, 16), PAIR)
+            xg[here, 0:TILE] = low[:, 512:HALF]
+            xg[here, TILE:HALF] = low[:, 0:512]
+            xg[here, HALF:HALF + 512] = high[:, 0:512]
+            xg[here, HALF + 512:2 * HALF] = high[:, 512:HALF]
         for tile in range(8):
             nb[rows, tile * TILE:(tile + 1) * TILE] = lax.dot_general(
                 xg[rows, tile * TILE:tile * TILE + 3 * TILE], band[tile],
@@ -553,7 +538,8 @@
             pltpu.VMEM((1, 1024), F32),
             pltpu.VMEM((32, 1024), BF16),
             pltpu.VMEM((COLS, 1024), F32),
-            pltpu.VMEM((PAIR, HALF), F32),
+            pltpu.VMEM((PAIR, TILE), F32),
+            pltpu.VMEM((1536, HALF), BF16),
             pltpu.VMEM((768, 1280), BF16),
             pltpu.VMEM((768, 1024), BF16),
             pltpu.VMEM((8, TILE, 384), BF16),

time: 63.5 us -> 64.9 us (1.022)
  Pallas kernels: 62.7 us -> 64.2 us
    pallas_call x1, Pallas kernels: 62 us -> 63.4 us  [shards(): pl.pallas_call(kernel, out_shape=OUTS, in_specs=[hbm] * 8, out_specs=(vme...]
where the time goes in v7:
time: 64.9 us; the launch traced here: 64.8 us
  Pallas kernels  64.2 us (99%)
    pallas_call x1, Pallas kernels, shards(): pl.pallas_call(kernel, out_shape=OUTS, in_specs=[hbm] * 8, out_specs=(vme...  63.4 us

profile of v7, /device:TPU:1, one launch (start us, length us, event | category | flops | bytes accessed | tf_op | source)
XLA Modules:
  0.0 64.8 jit_solution(5423380176141874916)
XLA Ops:
  0.6 63.4 %shard_map.111 = (bf16[32,1024]{1,0:T(8,128)(2,1)S(1)}, f32[24,1024]{1,0:T(8,128)S(1)}, f32[24,1024]{1,0:T(8,128)S(1)}, f32[1,1024]{1,0:T(1,128)S(1)}) custom-call(bf16[24,1024]{1,0:T(8,128)(2,1)} %bitcast.3, bf16[8,128,256]{2,1,0:T(8,128)(2,1)} %adj_h.1, s32[8]{0:T(128)} %off_h.1, s32[8]{0:T(128)} %live_h.1, bf16[24,1024]{1,0:T(8,128)(2,1)} %ws_h.1, ...), custom_call_target="tpu_custom_call" | custom-call | flops 1000000000 | bytes 10000000 | tf_op jit(solution)/shard_map/pallas_call | solution.py:526
  64.1 0.7 %shard_map.112 = (bf16[32,1024]{1,0:T(8,128)(2,1)}, f32[24,1024]{1,0:T(8,128)}, f32[24,1024]{1,0:T(8,128)}, f32[1,1024]{1,0:T(1,128)}) custom-call(bf16[32,1024]{1,0:T(8,128)(2,1)S(1)} %get-tuple-element.12.hid, f32[24,1024]{1,0:T(8,128)S(1)} %get-tuple-element.13.gs, f32[24,1024]{1,0:T(8,128)S(1)} %get-tuple-element.14.gn, f32[1,1024]{1,0:T(1,128)S(1)} %get-tuple-element.15.gb), custom_call_target="tpu_custom_call" | custom-call | tf_op jit(solution)/shard_map/pallas_call | solution.py:564

commit v8 on v6

--- a/solution.py
+++ b/solution.py
@@ -28,7 +28,7 @@
     feat_h, adj_h, off_h, live_h, ws_h, wn_h, bias_h, tgt_h,
     hid, gs_o, gn_o, gb_o,
     feat, adj, off, live, ws, wn, bias, tgt,
-    wide, stage, xg, nb, band, wsend, wg, wt, pre_acc, rsend, ra, rbs, rb, fg,
+    wide, stage, xg, nb, band, wsend, wg, wt, pre_acc, both, rsend, ra, rbs, rb, fg,
     in_sem, send_sem, recv_sem,
 ):
     loads = [
@@ -300,16 +300,15 @@
         dense = adj[tile].astype(F32)
         padded = jnp.concatenate([dense, jnp.zeros((TILE, TILE), F32)], 1)
         moved = pltpu.roll(padded, off[tile] - tile * TILE, 1)
-        band[tile] = (moved * live[tile].astype(F32)).astype(BF16)
+        band[tile] = (moved * live[tile].astype(F32)).T.astype(BF16)
 
     def neighbours(bz):
         col = mod4(bz)
         rows = pl.ds(pl.multiple_of(col * COLUMN, 16), COLUMN)
         await_bytes(xg.at[rows, pl.ds(pl.multiple_of(other * HALF, 128), HALF)], r_pair + col)
         for tile in range(8):
-            nb[rows, tile * TILE:(tile + 1) * TILE] = lax.dot_general(
-                xg[rows, tile * TILE:tile * TILE + 3 * TILE], band[tile],
-                (((1,), (1,)), ((), ())), preferred_element_type=F32,
+            nb[rows, tile * TILE:(tile + 1) * TILE] = jnp.dot(
+                xg[rows, tile * TILE:tile * TILE + 3 * TILE], band[tile], preferred_element_type=F32
             ).astype(BF16)
 
     def products(bz):
@@ -396,10 +395,8 @@
     hid[...] = act.astype(BF16)
     delta = (act - tgt[...].astype(F32)) * (gate * (1.0 + pre * (1.0 - gate))) * (1.0 / 128.0)
 
-    head = delta.astype(BF16)
-    rest = (delta - head.astype(F32)).astype(BF16)
-    both = jnp.concatenate([head] * 4 + [rest] * 4, 0)
-    turn = (((1,), (1,)), ((), ()))
+    head = delta.astype(BF16).astype(F32)
+    both[...] = jnp.concatenate([head, delta - head] * 2, 0).T.astype(BF16)
     bias_term = jnp.sum(delta, axis=1, keepdims=True)
     quarter = lax.div(lax.broadcasted_iota(jnp.int32, (PAIR, 128), 1), 32)
     blank = jnp.zeros((16, 128), F32)
@@ -420,8 +417,8 @@
         left = jnp.concatenate(
             [xg[span, TILE:TILE + 1024] for span in spans] + [nb[span, :] for span in spans], 0
         )
-        grad = lax.dot_general(left, both, turn, preferred_element_type=F32)
-        grad = grad[:, 0:128] + grad[:, 128:256]
+        grad = jnp.dot(left, both[...], preferred_element_type=F32)
+        grad = grad + pltpu.roll(grad, 32, 1)
 
         def packed(first):
             parts = [grad[first + col * PAIR:first + (col + 1) * PAIR] for col in range(4)]
@@ -556,11 +553,12 @@
             pltpu.VMEM((PAIR, HALF), F32),
             pltpu.VMEM((768, 1280), BF16),
             pltpu.VMEM((768, 1024), BF16),
-            pltpu.VMEM((8, TILE, 384), BF16),
+            pltpu.VMEM((8, 384, TILE), BF16),
             pltpu.VMEM((16, 32, 128), BF16),
             pltpu.VMEM((2, 16, 32, 128), BF16),
             pltpu.VMEM((4, 128, COLUMN), BF16),
             pltpu.VMEM((32, 1024), F32),
+            pltpu.VMEM((1024, 128), BF16),
             pltpu.VMEM((4, 4, 32, 128), BF16),
             pltpu.VMEM((4, 4, 32, 128), BF16),
             pltpu.VMEM((4, 2, 16, 128), BF16),

time: 63.5 us -> 64.1 us (level)
  Pallas kernels: 62.7 us -> 63.4 us
    pallas_call x1, Pallas kernels: 62 us -> 62.6 us  [shards(): pl.pallas_call(kernel, out_shape=OUTS, in_specs=[hbm] * 8, out_specs=(vme...]
where the time goes in v8:
time: 64.1 us; the launch traced here: 64 us
  Pallas kernels  63.4 us (99%)
    pallas_call x1, Pallas kernels, shards(): pl.pallas_call(kernel, out_shape=OUTS, in_specs=[hbm] * 8, out_specs=(vme...  62.6 us

profile of v8, /device:TPU:1, one launch (start us, length us, event | category | flops | bytes accessed | tf_op | source)
XLA Modules:
  0.0 64.0 jit_solution(6272647981952878249)
XLA Ops:
  0.6 62.6 %shard_map.111 = (bf16[32,1024]{1,0:T(8,128)(2,1)S(1)}, f32[24,1024]{1,0:T(8,128)S(1)}, f32[24,1024]{1,0:T(8,128)S(1)}, f32[1,1024]{1,0:T(1,128)S(1)}) custom-call(bf16[24,1024]{1,0:T(8,128)(2,1)} %bitcast.3, bf16[8,128,256]{2,1,0:T(8,128)(2,1)} %adj_h.1, s32[8]{0:T(128)} %off_h.1, s32[8]{0:T(128)} %live_h.1, bf16[24,1024]{1,0:T(8,128)(2,1)} %ws_h.1, ...), custom_call_target="tpu_custom_call" | custom-call | flops 1000000000 | bytes 10000000 | tf_op jit(solution)/shard_map/pallas_call | solution.py:538
  63.3 0.7 %shard_map.112 = (bf16[32,1024]{1,0:T(8,128)(2,1)}, f32[24,1024]{1,0:T(8,128)}, f32[24,1024]{1,0:T(8,128)}, f32[1,1024]{1,0:T(1,128)}) custom-call(bf16[32,1024]{1,0:T(8,128)(2,1)S(1)} %get-tuple-element.12.hid, f32[24,1024]{1,0:T(8,128)S(1)} %get-tuple-element.13.gs, f32[24,1024]{1,0:T(8,128)S(1)} %get-tuple-element.14.gn, f32[1,1024]{1,0:T(1,128)S(1)} %get-tuple-element.15.gb), custom_call_target="tpu_custom_call" | custom-call | tf_op jit(solution)/shard_map/pallas_call | solution.py:576

commit v9 on v6

--- a/solution.py
+++ b/solution.py
@@ -86,6 +86,7 @@
     r_chip = mod4(x - y) * 4 + zl
     for step in range(1, 4):
         tell(device(g, w_src_y * 4 + mod4(zh + step), c))
+        tell(device(g - x + mod4(x + step), p, other))
         tell(device(mod4(zl + step) * 4 + y, r_chip, 0))
         tell(device(mod4(zl + step) * 4 + y, r_chip, 1))
 
@@ -125,7 +126,7 @@
             stage[:, 512:HALF] = jnp.zeros((PAIR, TILE), F32)
 
     waits = (
-        6 + 3 + 7 + 15
+        6 + 3 + 7 + 15 + 3
         + (x != 0).astype(jnp.int32)
         + jnp.logical_not(stays).astype(jnp.int32)
         + (g < 15).astype(jnp.int32)
@@ -337,10 +338,12 @@
     def _():
         await_bytes(wg.at[c, w_src_y * 4 + zh], r_w1)
 
-    r_w2 = slot(1, 4)
+    r_w2 = slot(1, 2)
     part_w = wg.at[c, pl.ds(w_src_y * 4, 4)]
+    copy(part_w, part_w, partner, r_w2 + c)
     for step in range(1, 4):
-        copy(part_w, part_w, device(g - x + mod4(x + step), p, c), r_w2 + step)
+        for core in range(2):
+            copy(part_w, part_w, device(g - x + mod4(x + step), p, core), r_w2 + c)
 
     take_y2(0)
     await_bytes(block(y, zh + sign, "b"), r_z1 + 1)
@@ -351,10 +354,6 @@
     share(y, zh - sign, "all")
     share(y, zh + sign, "all")
     neighbours(zh)
-    for step in range(1, 4):
-        await_bytes(wg.at[c, pl.ds(mod4(y + x - step) * 4, 4)], r_w2 + step)
-    r_w3 = slot(1)
-    copy(wg.at[c], wg.at[c], partner, r_w3)
     take_y1(1)
     take_y1(2)
     await_bytes(block(y, zh + 2, "a"), r_z2)
@@ -364,7 +363,13 @@
     take_y2(2)
     take_y2(1)
 
-    await_bytes(wg.at[other], r_w3)
+    neighbours(zh - 1)
+    neighbours(zh + 1)
+    take_y3("a")
+    take_y3("b")
+
+    await_bytes(wg.at[other], r_w2 + other)
+    await_bytes(wg.at[c, 0:12], r_w2 + c)
     for col in range(4):
         rows = []
         for row in range(4):
@@ -380,12 +385,8 @@
     )
     pre_acc[...] = jnp.broadcast_to(bias_own, (32, 1024))
     products(zh)
-    neighbours(zh - 1)
-    neighbours(zh + 1)
     products(zh - 1)
     products(zh + 1)
-    take_y3("a")
-    take_y3("b")
     neighbours(zh + 2)
     products(zh + 2)
 

time: 63.5 us -> 63.3 us (level)
  no operation moved by 1% of the time
where the time goes in v9:
time: 63.3 us; the launch traced here: 63.1 us
  Pallas kernels  62.5 us (99%)
  between operations  0.64 us (1%)
    pallas_call x1, Pallas kernels, shards(): pl.pallas_call(kernel, out_shape=OUTS, in_specs=[hbm] * 8, out_specs=(vme...  61.7 us

profile of v9, /device:TPU:1, one launch (start us, length us, event | category | flops | bytes accessed | tf_op | source)
XLA Modules:
  0.0 63.1 jit_solution(1922362531155256481)
XLA Ops:
  0.6 61.7 %shard_map.111 = (bf16[32,1024]{1,0:T(8,128)(2,1)S(1)}, f32[24,1024]{1,0:T(8,128)S(1)}, f32[24,1024]{1,0:T(8,128)S(1)}, f32[1,1024]{1,0:T(1,128)S(1)}) custom-call(bf16[24,1024]{1,0:T(8,128)(2,1)} %bitcast.3, bf16[8,128,256]{2,1,0:T(8,128)(2,1)} %adj_h.1, s32[8]{0:T(128)} %off_h.1, s32[8]{0:T(128)} %live_h.1, bf16[24,1024]{1,0:T(8,128)(2,1)} %ws_h.1, ...), custom_call_target="tpu_custom_call" | custom-call | flops 1000000000 | bytes 10000000 | tf_op jit(solution)/shard_map/pallas_call | solution.py:542
  62.4 0.7 %shard_map.112 = (bf16[32,1024]{1,0:T(8,128)(2,1)}, f32[24,1024]{1,0:T(8,128)}, f32[24,1024]{1,0:T(8,128)}, f32[1,1024]{1,0:T(1,128)}) custom-call(bf16[32,1024]{1,0:T(8,128)(2,1)S(1)} %get-tuple-element.12.hid, f32[24,1024]{1,0:T(8,128)S(1)} %get-tuple-element.13.gs, f32[24,1024]{1,0:T(8,128)S(1)} %get-tuple-element.14.gn, f32[1,1024]{1,0:T(1,128)S(1)} %get-tuple-element.15.gb), custom_call_target="tpu_custom_call" | custom-call | tf_op jit(solution)/shard_map/pallas_call | solution.py:579

commit v10 on v9

--- a/solution.py
+++ b/solution.py
@@ -156,6 +156,10 @@
         @pl.when(jnp.logical_not(skip))
         def _():
             made.start()
+
+    def drain(first, last):
+        for made in sent[first:last]:
+            made.wait_send()
 
     def await_bytes(ref, recv):
         pltpu.make_async_copy(ref, ref, recv_sem.at[recv]).wait()
@@ -440,6 +444,21 @@
         if turn_of < 4:
             copy(rsend.at[row], ra.at[turn_of], device(g - x + row, p, c), r_ra + turn_of)
 
+    before_x = len(sent) - 3
+    drain(0, before_x)
+
+    @pl.when(g < 15)
+    def _():
+        halo_up.wait_send()
+
+    @pl.when(g > 0)
+    def _():
+        halo_down.wait_send()
+
+    @pl.when(x != 0)
+    def _():
+        w_zero.wait_send()
+
     for turn_of in range(1, 4):
         await_bytes(ra.at[turn_of], r_ra + turn_of)
 
@@ -468,6 +487,7 @@
     def _():
         pltpu.make_async_copy(rbs.at[zh, c], rb.at[zl, c], recv_sem.at[r_rb]).start()
 
+    drain(before_x, None)
     await_bytes(rb, r_rb)
     for core in range(2):
         total = (rb[0, core].astype(F32) + rb[1, core].astype(F32)) + (
@@ -477,11 +497,20 @@
             total, total[:, 48:49] + total[:, 49:50], total[:, 112:113] + total[:, 113:114]
         ).astype(BF16)
 
-    r_r2 = slot(1, 4)
+    r_r2, s_r2 = slot(1, 4), slot(0)
     for step in range(1, 16):
         far = lax.rem(g + step, 16)
-        copy(fg.at[r_chip], fg.at[r_chip], device(far, p, c), r_r2 + mod4(x - lax.rem(far, 4)))
+        remote(
+            fg.at[r_chip], fg.at[r_chip], device(far, p, c), s_r2, r_r2 + mod4(x - lax.rem(far, 4))
+        ).start()
+
+    @pl.when(jnp.logical_not(stays))
+    def _():
+        r_zero.wait_send()
+
     for k in (0, 1, 3, 2):
+        if k == 2:
+            pltpu.make_async_copy(fg.at[0:15], fg.at[0:15], send_sem.at[s_r2]).wait()
         await_bytes(fg.at[0:(4 if k else 3)], r_r2 + k)
         for half in range(2):
             part = lax.rem(x - y + k + 4, 4) * 2 + half
@@ -495,25 +524,6 @@
             gs_o[:, span] = turned[0:24]
             gn_o[:, span] = turned[24:48]
             gb_o[:, span] = turned[48:49] + turned[49:50]
-
-    for made in sent:
-        made.wait_send()
-
-    @pl.when(g < 15)
-    def _():
-        halo_up.wait_send()
-
-    @pl.when(g > 0)
-    def _():
-        halo_down.wait_send()
-
-    @pl.when(x != 0)
-    def _():
-        w_zero.wait_send()
-
-    @pl.when(jnp.logical_not(stays))
-    def _():
-        r_zero.wait_send()
 
     assert used[0] <= SENDS and used[1] <= RECVS, used
 

time: 63.3 us -> 63.1 us (level)
  no operation moved by 1% of the time
where the time goes in v10:
time: 63.1 us; the launch traced here: 63 us
  Pallas kernels  62.3 us (99%)
  between operations  0.64 us (1%)
    pallas_call x1, Pallas kernels, shards(): pl.pallas_call(kernel, out_shape=OUTS, in_specs=[hbm] * 8, out_specs=(vme...  61.6 us

profile of v10, /device:TPU:1, one launch (start us, length us, event | category | flops | bytes accessed | tf_op | source)
XLA Modules:
  0.0 63.0 jit_solution(7453849884132392686)
XLA Ops:
  0.6 61.6 %shard_map.111 = (bf16[32,1024]{1,0:T(8,128)(2,1)S(1)}, f32[24,1024]{1,0:T(8,128)S(1)}, f32[24,1024]{1,0:T(8,128)S(1)}, f32[1,1024]{1,0:T(1,128)S(1)}) custom-call(bf16[24,1024]{1,0:T(8,128)(2,1)} %bitcast.3, bf16[8,128,256]{2,1,0:T(8,128)(2,1)} %adj_h.1, s32[8]{0:T(128)} %off_h.1, s32[8]{0:T(128)} %live_h.1, bf16[24,1024]{1,0:T(8,128)(2,1)} %ws_h.1, ...), custom_call_target="tpu_custom_call" | custom-call | flops 1000000000 | bytes 10000000 | tf_op jit(solution)/shard_map/pallas_call | solution.py:552
  62.2 0.7 %shard_map.112 = (bf16[32,1024]{1,0:T(8,128)(2,1)}, f32[24,1024]{1,0:T(8,128)}, f32[24,1024]{1,0:T(8,128)}, f32[1,1024]{1,0:T(1,128)}) custom-call(bf16[32,1024]{1,0:T(8,128)(2,1)S(1)} %get-tuple-element.12.hid, f32[24,1024]{1,0:T(8,128)S(1)} %get-tuple-element.13.gs, f32[24,1024]{1,0:T(8,128)S(1)} %get-tuple-element.14.gn, f32[1,1024]{1,0:T(1,128)S(1)} %get-tuple-element.15.gb), custom_call_target="tpu_custom_call" | custom-call | tf_op jit(solution)/shard_map/pallas_call | solution.py:589

commit v11 on v10

--- a/solution.py
+++ b/solution.py
@@ -58,7 +58,6 @@
     partner = device(g, p, other)
     y_fwd = device(g, mod4(y + sign) * 4 + zh, c)
     y_bwd = device(g, mod4(y - sign) * 4 + zh, c)
-    y_far = device(g, mod4(y + 2) * 4 + zh, c)
     z_fwd = device(g, y * 4 + mod4(zh + sign), c)
     z_bwd = device(g, y * 4 + mod4(zh - sign), c)
     stays = jnp.logical_and(zh == zl, jnp.logical_and(x == 0, y == 0))
@@ -78,7 +77,7 @@
         tell(device(g + 1, p, 0))
         tell(device(g + 1, p, 1))
 
-    for target in (z_fwd, z_bwd, y_fwd, y_bwd, y_far, partner):
+    for target in (z_fwd, z_bwd, y_fwd, y_bwd, partner):
         tell(target)
 
     w_src_y = mod4(y + x)
@@ -126,7 +125,7 @@
             stage[:, 512:HALF] = jnp.zeros((PAIR, TILE), F32)
 
     waits = (
-        6 + 3 + 7 + 15 + 3
+        5 + 3 + 7 + 15 + 3
         + (x != 0).astype(jnp.int32)
         + jnp.logical_not(stays).astype(jnp.int32)
         + (g < 15).astype(jnp.int32)
@@ -232,12 +231,11 @@
 
     r_z1 = slot(1, 4)
     r_z2 = slot(1, 2)
-    r_y1 = slot(1, 12)
-    r_y2 = slot(1, 6)
-    r_y3 = slot(1, 6)
+    r_y1 = slot(1, 16)
+    r_y2 = slot(1, 8)
 
     def column(number):
-        return zh + sign * (0, -1, 1)[number]
+        return zh + 2 if number == 3 else zh + sign * (0, -1, 1)[number]
 
     def send_y1(number, part):
         first = r_y1 + 4 * number + (0 if part == "a" else 2)
@@ -262,19 +260,6 @@
         share(y + 2, bz, "a")
         await_bytes(block(y + 2, bz, "b"), r_y2 + 2 * number + 1)
         share(y + 2, bz, "b")
-
-    def send_y3(part):
-        first = r_y3 + (0 if part == "a" else 3)
-        forward(y, zh + 2, part, y_fwd, first)
-        forward(y, zh + 2, part, y_bwd, first + 1)
-        forward(y, zh + 2, part, y_far, first + 2)
-        share(y, zh + 2, part)
-
-    def take_y3(part):
-        first = r_y3 + (0 if part == "a" else 3)
-        for offset, by in enumerate((y - sign, y + sign, y + 2)):
-            await_bytes(block(by, zh + 2, part), first + offset)
-            share(by, zh + 2, part)
 
     await_bytes(stage.at[other_rows, pl.ds(pl.multiple_of(other * TILE, 128), 512)], r_swap)
     block(y, zh, "a")[...] = stage[:, pl.ds(pl.multiple_of(other * PART_B, 128), PART_A)].astype(BF16)
@@ -361,16 +346,16 @@
     take_y1(1)
     take_y1(2)
     await_bytes(block(y, zh + 2, "a"), r_z2)
-    send_y3("a")
+    send_y1(3, "a")
     await_bytes(block(y, zh + 2, "b"), r_z2 + 1)
-    send_y3("b")
+    send_y1(3, "b")
+    share(y, zh + 2, "all")
     take_y2(2)
     take_y2(1)
-
     neighbours(zh - 1)
+    take_y1(3)
     neighbours(zh + 1)
-    take_y3("a")
-    take_y3("b")
+    take_y2(3)
 
     await_bytes(wg.at[other], r_w2 + other)
     await_bytes(wg.at[c, 0:12], r_w2 + c)

time: 63.1 us -> 64.9 us (1.029)
  Pallas kernels: 62.3 us -> 64.1 us
    pallas_call x1, Pallas kernels: 61.6 us -> 63.4 us  [shards(): pl.pallas_call(kernel, out_shape=OUTS, in_specs=[hbm] * 8, out_specs=(vme...]
where the time goes in v11:
time: 64.9 us; the launch traced here: 64.8 us
  Pallas kernels  64.1 us (99%)
    pallas_call x1, Pallas kernels, shards(): pl.pallas_call(kernel, out_shape=OUTS, in_specs=[hbm] * 8, out_specs=(vme...  63.4 us

profile of v11, /device:TPU:1, one launch (start us, length us, event | category | flops | bytes accessed | tf_op | source)
XLA Modules:
  0.0 64.8 jit_solution(13988453605618048165)
XLA Ops:
  0.6 63.4 %shard_map.111 = (bf16[32,1024]{1,0:T(8,128)(2,1)S(1)}, f32[24,1024]{1,0:T(8,128)S(1)}, f32[24,1024]{1,0:T(8,128)S(1)}, f32[1,1024]{1,0:T(1,128)S(1)}) custom-call(bf16[24,1024]{1,0:T(8,128)(2,1)} %bitcast.3, bf16[8,128,256]{2,1,0:T(8,128)(2,1)} %adj_h.1, s32[8]{0:T(128)} %off_h.1, s32[8]{0:T(128)} %live_h.1, bf16[24,1024]{1,0:T(8,128)(2,1)} %ws_h.1, ...), custom_call_target="tpu_custom_call" | custom-call | flops 1000000000 | bytes 10000000 | tf_op jit(solution)/shard_map/pallas_call | solution.py:537
  64.0 0.7 %shard_map.112 = (bf16[32,1024]{1,0:T(8,128)(2,1)}, f32[24,1024]{1,0:T(8,128)}, f32[24,1024]{1,0:T(8,128)}, f32[1,1024]{1,0:T(1,128)}) custom-call(bf16[32,1024]{1,0:T(8,128)(2,1)S(1)} %get-tuple-element.12.hid, f32[24,1024]{1,0:T(8,128)S(1)} %get-tuple-element.13.gs, f32[24,1024]{1,0:T(8,128)S(1)} %get-tuple-element.14.gn, f32[1,1024]{1,0:T(1,128)S(1)} %get-tuple-element.15.gb), custom_call_target="tpu_custom_call" | custom-call | tf_op jit(solution)/shard_map/pallas_call | solution.py:574

commit v12 on v10

--- a/solution.py
+++ b/solution.py
@@ -279,7 +279,6 @@
     await_bytes(stage.at[other_rows, pl.ds(pl.multiple_of(other * TILE, 128), 512)], r_swap)
     block(y, zh, "a")[...] = stage[:, pl.ds(pl.multiple_of(other * PART_B, 128), PART_A)].astype(BF16)
     forward(y, zh, "a", z_fwd, r_z1)
-    forward(y, zh, "a", z_bwd, r_z1 + 3)
     send_y1(0, "a")
 
     @pl.when(jnp.logical_and(c == 0, g > 0))
@@ -294,6 +293,7 @@
 
     block(y, zh, "b")[...] = stage[:, pl.ds(pl.multiple_of(c * PART_A, 128), PART_B)].astype(BF16)
     forward(y, zh, "b", z_bwd, r_z1 + 1)
+    forward(y, zh, "a", z_bwd, r_z1 + 3)
     forward(y, zh, "b", z_fwd, r_z1 + 2)
 
     send_y1(0, "b")
@@ -332,8 +332,9 @@
     await_bytes(block(y, zh - sign, "a"), r_z1)
     forward(y, zh - sign, "a", z_fwd, r_z2)
     send_y1(1, "a")
-    await_bytes(block(y, zh + sign, "a"), r_z1 + 3)
-    send_y1(2, "a")
+    await_bytes(block(y, zh + sign, "b"), r_z1 + 1)
+    forward(y, zh + sign, "b", z_bwd, r_z2 + 1)
+    send_y1(2, "b")
 
     for step in range(1, 4):
         await_bytes(wg.at[c, w_src_y * 4 + mod4(zh + step)], r_w1 + 4 - step)
@@ -350,9 +351,8 @@
             copy(part_w, part_w, device(g - x + mod4(x + step), p, core), r_w2 + c)
 
     take_y2(0)
-    await_bytes(block(y, zh + sign, "b"), r_z1 + 1)
-    forward(y, zh + sign, "b", z_bwd, r_z2 + 1)
-    send_y1(2, "b")
+    await_bytes(block(y, zh + sign, "a"), r_z1 + 3)
+    send_y1(2, "a")
     await_bytes(block(y, zh - sign, "b"), r_z1 + 2)
     send_y1(1, "b")
     share(y, zh - sign, "all")

time: 63.1 us -> 64.4 us (1.021)
  Pallas kernels: 62.3 us -> 63.6 us
    pallas_call x1, Pallas kernels: 61.6 us -> 62.9 us  [shards(): pl.pallas_call(kernel, out_shape=OUTS, in_specs=[hbm] * 8, out_specs=(vme...]
where the time goes in v12:
time: 64.4 us; the launch traced here: 64.3 us
  Pallas kernels  63.6 us (99%)
    pallas_call x1, Pallas kernels, shards(): pl.pallas_call(kernel, out_shape=OUTS, in_specs=[hbm] * 8, out_specs=(vme...  62.9 us

profile of v12, /device:TPU:1, one launch (start us, length us, event | category | flops | bytes accessed | tf_op | source)
XLA Modules:
  0.0 64.3 jit_solution(10031942809539239237)
XLA Ops:
  0.6 62.9 %shard_map.111 = (bf16[32,1024]{1,0:T(8,128)(2,1)S(1)}, f32[24,1024]{1,0:T(8,128)S(1)}, f32[24,1024]{1,0:T(8,128)S(1)}, f32[1,1024]{1,0:T(1,128)S(1)}) custom-call(bf16[24,1024]{1,0:T(8,128)(2,1)} %bitcast.3, bf16[8,128,256]{2,1,0:T(8,128)(2,1)} %adj_h.1, s32[8]{0:T(128)} %off_h.1, s32[8]{0:T(128)} %live_h.1, bf16[24,1024]{1,0:T(8,128)(2,1)} %ws_h.1, ...), custom_call_target="tpu_custom_call" | custom-call | flops 1000000000 | bytes 10000000 | tf_op jit(solution)/shard_map/pallas_call | solution.py:552
  63.5 0.7 %shard_map.112 = (bf16[32,1024]{1,0:T(8,128)(2,1)}, f32[24,1024]{1,0:T(8,128)}, f32[24,1024]{1,0:T(8,128)}, f32[1,1024]{1,0:T(1,128)}) custom-call(bf16[32,1024]{1,0:T(8,128)(2,1)S(1)} %get-tuple-element.12.hid, f32[24,1024]{1,0:T(8,128)S(1)} %get-tuple-element.13.gs, f32[24,1024]{1,0:T(8,128)S(1)} %get-tuple-element.14.gn, f32[1,1024]{1,0:T(1,128)S(1)} %get-tuple-element.15.gb), custom_call_target="tpu_custom_call" | custom-call | tf_op jit(solution)/shard_map/pallas_call | solution.py:589

commit v13 on v10

--- a/solution.py
+++ b/solution.py
@@ -368,8 +368,8 @@
     take_y2(1)
 
     neighbours(zh - 1)
+    take_y3("a")
     neighbours(zh + 1)
-    take_y3("a")
     take_y3("b")
 
     await_bytes(wg.at[other], r_w2 + other)

time: 63.1 us -> 63 us (level)
  no operation moved by 1% of the time
where the time goes in v13:
time: 63 us; the launch traced here: 62.8 us
  Pallas kernels  62.2 us (99%)
  between operations  0.64 us (1%)
    pallas_call x1, Pallas kernels, shards(): pl.pallas_call(kernel, out_shape=OUTS, in_specs=[hbm] * 8, out_specs=(vme...  61.5 us

profile of v13, /device:TPU:1, one launch (start us, length us, event | category | flops | bytes accessed | tf_op | source)
XLA Modules:
  0.0 62.8 jit_solution(6992425140083150259)
XLA Ops:
  0.6 61.5 %shard_map.111 = (bf16[32,1024]{1,0:T(8,128)(2,1)S(1)}, f32[24,1024]{1,0:T(8,128)S(1)}, f32[24,1024]{1,0:T(8,128)S(1)}, f32[1,1024]{1,0:T(1,128)S(1)}) custom-call(bf16[24,1024]{1,0:T(8,128)(2,1)} %bitcast.3, bf16[8,128,256]{2,1,0:T(8,128)(2,1)} %adj_h.1, s32[8]{0:T(128)} %off_h.1, s32[8]{0:T(128)} %live_h.1, bf16[24,1024]{1,0:T(8,128)(2,1)} %ws_h.1, ...), custom_call_target="tpu_custom_call" | custom-call | flops 1000000000 | bytes 10000000 | tf_op jit(solution)/shard_map/pallas_call | solution.py:552
  62.1 0.7 %shard_map.112 = (bf16[32,1024]{1,0:T(8,128)(2,1)}, f32[24,1024]{1,0:T(8,128)}, f32[24,1024]{1,0:T(8,128)}, f32[1,1024]{1,0:T(1,128)}) custom-call(bf16[32,1024]{1,0:T(8,128)(2,1)S(1)} %get-tuple-element.12.hid, f32[24,1024]{1,0:T(8,128)S(1)} %get-tuple-element.13.gs, f32[24,1024]{1,0:T(8,128)S(1)} %get-tuple-element.14.gn, f32[1,1024]{1,0:T(1,128)S(1)} %get-tuple-element.15.gb), custom_call_target="tpu_custom_call" | custom-call | tf_op jit(solution)/shard_map/pallas_call | solution.py:589
